TPU v7x, 32 devices: a whole 2x2x4 slice. The times are simulated.
32 devices in a mesh: inst: 4 (over y, x), tp: 8 (over z, core).
Axes of the slice: x: 2, y: 2, z: 4, core: 2. Of those that a mesh axis runs over, the one named last changes fastest.
Arguments:
- tokens: bfloat16 [640, 8192], P('inst'), as said below
- doc_ids: int32 [4, 160], replicated, may hold values from 0 to 3, never falling along the last dimension, each value on 1 to 80 neighbouring positions
- query_one: bfloat16 [8192, 1024], P('inst', 'tp'), as said below
- keyval_one: bfloat16 [8192, 256], P('inst', 'tp'), as said below
- output_one: bfloat16 [1024, 8192], P('tp', 'inst'), may hold values from -0.1875 to 0.1875
- query_two: bfloat16 [8192, 1024], P('inst', 'tp'), as said below
- keyval_two: bfloat16 [8192, 256], P('inst', 'tp'), as said below
- output_two: bfloat16 [1024, 8192], P('tp', 'inst'), may hold values from -0.25 to 0.25
Outputs:
- blended: bfloat16 [640, 8192], P('inst', 'tp')
Inputs may be any that keep to these rules, and one draw needn't show every extreme that they name: `doc_ids`: along each row the document numbers never fall; each document holds 1 to 80 positions. `query_one`: A projection scaled by the square root of its fan-in. `keyval_one`: A projection scaled by the square root of its fan-in. `query_two`: A projection scaled by the square root of its fan-in. `keyval_two`: A projection scaled by the square root of its fan-in. `tokens`: hidden rows of order one.
All inputs are finite; a program needn't handle non-finite values.
Results may differ from a plain program's by a relative error of at most 0.034.
Values may be sent and summed in bfloat16 or wider, within the bound.
No kernel may reach another device: no remote copies, remote signals or barrier semaphores. Data moves between devices by JAX's collectives and lax.ppermute only.
A program may use at most 64 MiB of HBM per device.

v0:
```python
import jax
import jax.numpy as jnp
from jax import lax
from jax.sharding import PartitionSpec as P

GROUP = 8


def from_partner(block, axis, bit):
    count = lax.axis_size(axis)
    route = []
    for low in range(count):
        high = low | 1 << bit
        if high != low and high < count:
            route += [(low, high), (high, low)]
    return lax.ppermute(block, axis, route)


def passed_along(block, axis, distance):
    devices = range(lax.axis_size(axis))
    route = [((i - distance) % len(devices), i) for i in devices]
    return lax.ppermute(block, axis, route)


def normalize(hidden):
    floats = hidden.astype(jnp.float32)
    scale = lax.rsqrt(jnp.mean(floats * floats, axis=1, keepdims=True) + 1e-06)
    return (floats * scale).astype(jnp.bfloat16)


def share_head(own_piece):
    gathered = own_piece
    group_rank = lax.axis_index("tp")
    for bit_level in range(GROUP.bit_length() - 1):
        partner = from_partner(gathered, "tp", bit_level)
        is_lower = group_rank // 2**bit_level % 2 == 0
        gathered = jnp.where(
            is_lower,
            jnp.concatenate([gathered, partner], 1),
            jnp.concatenate([partner, gathered], 1),
        )
    return gathered


def head_terms(hidden, doc_row, query_shard, keyval_shard, output_shard):
    normed = normalize(hidden)
    row_count = normed.shape[0]
    query_total = jnp.dot(
        normed,
        lax.all_gather(query_shard, "inst", axis=0, tiled=True),
        preferred_element_type=jnp.float32,
    )
    keyval_total = jnp.dot(
        normed,
        lax.all_gather(keyval_shard, "inst", axis=0, tiled=True),
        preferred_element_type=jnp.float32,
    )
    head_dim = query_shard.shape[1]
    queries = (query_total * head_dim ** (-0.5)).astype(jnp.bfloat16)
    keyvals = share_head(keyval_total.astype(jnp.bfloat16))
    key_rows = keyvals[:, :head_dim]
    value_rows = keyvals[:, head_dim:]
    scores = lax.dot_general(
        queries, key_rows, (((1,), (1,)), ((), ())), preferred_element_type=jnp.float32
    )
    position = jnp.arange(row_count)
    allowed = (doc_row[:, None] == doc_row[None, :]) & (position[None, :] <= position[:, None])
    scores = jnp.where(allowed, scores, -1e30)
    row_top = jnp.max(scores, axis=1, keepdims=True)
    weights = jnp.exp(scores - row_top)
    probabilities = (weights / jnp.sum(weights, axis=1, keepdims=True)).astype(jnp.bfloat16)
    context = jnp.dot(probabilities, value_rows, preferred_element_type=jnp.float32).astype(
        jnp.bfloat16
    )
    return jnp.dot(
        context,
        lax.all_gather(output_shard, "inst", axis=1, tiled=True),
        preferred_element_type=jnp.float32,
    )


def shards(tokens, doc_ids, query_one, keyval_one, output_one, query_two, keyval_two, output_two):
    inst_count = lax.axis_size("inst")
    inst_place = lax.axis_index("inst")
    own_docs = lax.dynamic_index_in_dim(doc_ids, inst_place, 0, keepdims=False)
    prev_docs = lax.dynamic_index_in_dim(
        doc_ids, (inst_place + inst_count - 1) % inst_count, 0, keepdims=False
    )
    first_terms = head_terms(tokens, own_docs, query_one, keyval_one, output_one)
    column_width = tokens.shape[1] // lax.axis_size("tp")
    tensor_rank = lax.axis_index("tp")
    summed = lax.psum(first_terms.astype(jnp.bfloat16), "tp").astype(jnp.float32)
    middle = (tokens.astype(jnp.float32) + summed).astype(jnp.bfloat16)
    arrived = passed_along(middle, "inst", 1)
    second_terms = head_terms(arrived, prev_docs, query_two, keyval_two, output_two)
    shares = lax.psum_scatter(
        second_terms.astype(jnp.bfloat16), "tp", scatter_dimension=1, tiled=True
    ).astype(jnp.float32)
    residual_part = lax.dynamic_slice_in_dim(arrived, tensor_rank * column_width, column_width, 1)
    return (residual_part.astype(jnp.float32) + shares).astype(jnp.bfloat16)


def solution(mesh):
    placed = (
        P("inst", None),
        P(),
        P("inst", "tp"),
        P("inst", "tp"),
        P("tp", "inst"),
        P("inst", "tp"),
        P("inst", "tp"),
        P("tp", "inst"),
    )
    return jax.shard_map(
        shards, mesh=mesh, in_specs=placed, out_specs=P("inst", "tp"), check_vma=False
    )
```

profile of v0, /device:TPU:1, one launch (start us, length us, event | category | flops | bytes accessed | tf_op | source)
XLA Modules:
  0.0 330.3 jit_solution(2186107995874115366)
XLA Ops:
  6.5 0.0 copy-start
  6.5 0.0 all-gather.5.cloned.1.call-start
  6.5 0.7 all-gather.5.cloned.1.call-update
  7.3 0.0 all-gather.7.cloned.1.call-start
  7.3 0.7 all-gather.7.cloned.1.call-update
  8.0 0.0 all-reduce.2.cloned.1.call-start
  8.1 9.8 %all_gather.19 = bf16[8192,32]{0,1:T(8,128)(2,1)S(1)} all-gather(bf16[2048,32]{0,1:T(8,128)(2,1)} %param.11), channel_id=1, replica_groups=mesh['inst'=4,'tp'=8] {'inst'}, dimensions={0}, use_global_device_ids=true | all-gather | bytes 655360 | tf_op jit(solution)/shard_map/all_gather | solution.py:55
  17.8 2.6 fusion.2
  20.4 0.0 copy-start.2
  20.4 0.0 copy-done
  20.4 1.0 convolution_convert_fusion.5
  21.4 2.0 collective-permute-start
  23.5 0.8 collective-permute-done
  24.3 1.4 collective-permute-start.1
  25.7 1.8 collective-permute-done.1
  27.6 2.4 collective-permute-start.2
  30.0 0.0 copy-done.2
  30.0 1.6 collective-permute-done.2
  31.7 14.9 %all-gather.5.cloned.1.call-done = bf16[8192,128]{1,0:T(8,128)(2,1)} async-done(((bf16[2048,128]{1,0:T(8,128)(2,1)}), bf16[8192,128]{1,0:T(8,128)(2,1)}) %all-gather.5.cloned.1.call-update) | async-done | bytes 2097168 | tf_op jit(solution)/shard_map/all_gather | solution.py:50
  46.6 2.7 fusion.35
  49.3 0.1 fusion.15
  49.4 34.5 %all-gather.7.cloned.1.call-done = bf16[128,8192]{1,0:T(8,128)(2,1)} async-done(((bf16[128,2048]{1,0:T(8,128)(2,1)}), bf16[128,8192]{1,0:T(8,128)(2,1)}) %all-gather.7.cloned.1.call-update) | async-done | bytes 2097168 | tf_op jit(solution)/shard_map/all_gather | solution.py:77
  83.8 4.1 %convolution_convert_fusion.1 = bf16[160,8192]{1,0:T(8,128)(2,1)} fusion(bf16[128,8192]{1,0:T(8,128)(2,1)} %all-gather.7.cloned.1.call-done, f32[160,160]{0,1:T(8,128)S(1)} %get-tuple-element.8, f32[160]{0:T(256)S(1)} %fusion.15, f32[160]{0:T(256)S(1)} %get-tuple-element.7, bf16[160,256]{0,1:T(8,128)(2,1)S(1)} %maximum_select_fusion), kind=kOutput, calls=%fused_computation.1 | convolution fusion | flops 343505920 | bytes 4950016 | tf_op jit(solution)/shard_map/dot_general | solution.py:75
  88.0 0.0 all-reduce.2.cloned.1.call-update
  88.0 0.0 all-gather.9.cloned.1.call-start
  88.0 0.5 all-gather.9.cloned.1.call-update
  88.6 0.0 copy-start.1
  88.6 0.0 all-gather.11.cloned.1.call-start
  88.6 67.5 %all-reduce.2.cloned.1.call-done = bf16[160,8192]{1,0:T(8,128)(2,1)} async-done(((bf16[160,8192]{1,0:T(8,128)(2,1)}), bf16[160,8192]{1,0:T(8,128)(2,1)}) %all-reduce.2.cloned.1.call-update) | async-done | bytes 2621456 | tf_op jit(solution)/shard_map/psum | solution.py:92
  156.2 4.1 %fusion.4 = bf16[160,8192]{1,0:T(8,128)(2,1)} fusion(bf16[160,8192]{1,0:T(8,128)(2,1)S(1)} %copy-done, bf16[160,8192]{1,0:T(8,128)(2,1)} %all-reduce.2.cloned.1.call-done), kind=kLoop, calls=%fused_computation.11 | loop fusion | flops 5242880 | bytes 7864320 | tf_op jit(solution)/shard_map/convert_element_type | solution.py:93
  160.2 1.2 collective-permute-start.3
  161.4 0.0 all-gather.11.cloned.1.call-update
  161.4 0.0 reduce-scatter.2.cloned.1.call-start
  161.5 0.0 copy-done.1
  161.5 66.9 %all_gather.22 = bf16[8192,32]{0,1:T(8,128)(2,1)S(1)} all-gather(bf16[2048,32]{0,1:T(8,128)(2,1)S(1)} %copy-done.1), channel_id=1, replica_groups=mesh['inst'=4,'tp'=8] {'inst'}, dimensions={0}, use_global_device_ids=true | all-gather | bytes 655360 | tf_op jit(solution)/shard_map/all_gather | solution.py:55
  228.4 0.0 collective-permute-done.3
  228.4 0.6 fusion
  229.0 1.0 convolution_convert_fusion.4
  230.1 2.8 collective-permute-start.4
  232.9 0.8 collective-permute-done.4
  233.7 1.5 collective-permute-start.5
  235.2 1.7 collective-permute-done.5
  237.0 2.3 collective-permute-start.6
  239.2 1.9 collective-permute-done.6
  241.1 4.2 %all-gather.9.cloned.1.call-done = bf16[8192,128]{1,0:T(8,128)(2,1)} async-done(((bf16[2048,128]{1,0:T(8,128)(2,1)}), bf16[8192,128]{1,0:T(8,128)(2,1)}) %all-gather.9.cloned.1.call-update) | async-done | bytes 2097168 | tf_op jit(solution)/shard_map/all_gather | solution.py:50
  245.3 2.7 fusion.38
  248.0 0.1 fusion.16
  248.1 34.3 %all-gather.11.cloned.1.call-done = bf16[128,8192]{1,0:T(8,128)(2,1)} async-done(((bf16[128,2048]{1,0:T(8,128)(2,1)}), bf16[128,8192]{1,0:T(8,128)(2,1)}) %all-gather.11.cloned.1.call-update) | async-done | bytes 2097168 | tf_op jit(solution)/shard_map/all_gather | solution.py:77
  282.4 4.2 %convolution_convert_fusion = bf16[160,8192]{1,0:T(8,128)(2,1)} fusion(bf16[128,8192]{1,0:T(8,128)(2,1)} %all-gather.11.cloned.1.call-done, f32[160,160]{0,1:T(8,128)S(1)} %get-tuple-element.10, f32[160]{0:T(256)S(1)} %fusion.16, f32[160]{0:T(256)S(1)} %get-tuple-element.9, bf16[160,256]{0,1:T(8,128)(2,1)S(1)} %maximum_select_fusion.1), kind=kOutput, calls=%fused_computation | convolution fusion | flops 343505920 | bytes 4950016 | tf_op jit(solution)/shard_map/dot_general | solution.py:75
  286.5 0.0 reduce-scatter.2.cloned.1.call-update
  286.6 35.1 %reduce-scatter.2.cloned.1.call-done = bf16[160,1024]{1,0:T(8,128)(2,1)} async-done(((bf16[160,8192]{1,0:T(8,128)(2,1)}), bf16[160,1024]{1,0:T(8,128)(2,1)}) %reduce-scatter.2.cloned.1.call-update) | async-done | bytes 327696 | tf_op jit(solution)/shard_map/reduce_scatter | solution.py:96
  321.6 1.8 add_convert_fusion
  (9 shorter events, 0.1 us)
Async XLA Ops:
  6.5 13.9 %copy-start = (bf16[160,8192]{1,0:T(8,128)(2,1)S(1)}, bf16[160,8192]{1,0:T(8,128)(2,1)}, u32[]{:S(2)}) copy-start(bf16[160,8192]{1,0:T(8,128)(2,1)} %param.8) | copy-start | bytes 7864324
  6.5 40.1 %all-gather.5.cloned.1.call-start = ((), (), s32[]{:S(2)}) async-start(), calls=%async_computation.1 | async-start | bytes 2621440 | tf_op jit(solution)/shard_map/all_gather | solution.py:50
  7.3 76.6 %all-gather.7.cloned.1.call-start = ((), (), s32[]{:S(2)}) async-start(), calls=%async_computation.2 | async-start | bytes 2621440 | tf_op jit(solution)/shard_map/all_gather | solution.py:77
  8.0 148.2 %all-reduce.2.cloned.1.call-start = ((), (), s32[]{:S(2)}) async-start(), calls=%async_computation.3 | async-start | bytes 5242880 | tf_op jit(solution)/shard_map/psum | solution.py:92
  20.4 9.6 %copy-start.2 = (s32[4,160]{1,0:T(4,128)S(1)}, s32[4,160]{1,0:T(4,128)}, u32[]{:S(2)}) copy-start(s32[4,160]{1,0:T(4,128)} %param.9) | copy-start | bytes 7684
  21.4 2.9 collective-permute-start
  24.3 3.2 collective-permute-start.1
  27.6 4.1 %collective-permute-start.2 = (bf16[160,128]{0,1:T(8,128)(2,1)S(1)}, bf16[160,128]{0,1:T(8,128)(2,1)S(1)}, u32[]{:S(2)}, u32[]{:S(2)}) collective-permute-start(bf16[160,128]{0,1:T(8,128)(2,1)S(1)} %maximum_select_fusion.2), channel_id=1, source_target_pairs={{0,4},{4,0},{1,5},{5,1},{2,6},{6,2},{3,7},{7,3},{8,12},{12,8},{9,1... | collective-permute-start | bytes 122888 | tf_op jit(solution)/shard_map/ppermute | solution.py:16
  88.0 157.3 %all-gather.9.cloned.1.call-start = ((), (), s32[]{:S(2)}) async-start(), calls=%async_computation.4 | async-start | bytes 2621440 | tf_op jit(solution)/shard_map/all_gather | solution.py:50
  88.6 72.9 %copy-start.1 = (bf16[2048,32]{0,1:T(8,128)(2,1)S(1)}, bf16[2048,32]{0,1:T(8,128)(2,1)}, u32[]{:S(2)}) copy-start(bf16[2048,32]{0,1:T(8,128)(2,1)} %param.14) | copy-start | bytes 393220
  88.6 193.8 %all-gather.11.cloned.1.call-start = ((), (), s32[]{:S(2)}) async-start(), calls=%async_computation.5 | async-start | bytes 2621440 | tf_op jit(solution)/shard_map/all_gather | solution.py:77
  160.2 68.2 %collective-permute-start.3 = (bf16[160,8192]{1,0:T(8,128)(2,1)}, bf16[160,8192]{1,0:T(8,128)(2,1)S(1)}, u32[]{:S(2)}, u32[]{:S(2)}) collective-permute-start(bf16[160,8192]{1,0:T(8,128)(2,1)} %fusion.4), channel_id=1, source_target_pairs={{24,0},{0,8},{8,16},{16,24},{25,1},{1,9},{9,17},{17,25},{26,2},{2,... | collective-permute-start | bytes 7864328 | tf_op jit(solution)/shard_map/ppermute | solution.py:22
  161.4 160.2 %reduce-scatter.2.cloned.1.call-start = ((), (), s32[]{:S(2)}) async-start(), calls=%async_computation.6 | async-start | bytes 2949120 | tf_op jit(solution)/shard_map/reduce_scatter | solution.py:96
  230.1 3.6 %collective-permute-start.4 = (bf16[160,32]{0,1:T(8,128)(2,1)S(1)}, bf16[160,32]{0,1:T(8,128)(2,1)S(1)}, u32[]{:S(2)}, u32[]{:S(2)}) collective-permute-start(bf16[160,32]{0,1:T(8,128)(2,1)S(1)} %convolution_convert_fusion.4), channel_id=1, source_target_pairs={{0,1},{1,0},{2,3},{3,2},{4,5},{5,4},{6,7},{7,6},{8,9},{9,8},{10,11... | collective-permute-start | bytes 30728 | tf_op jit(solution)/shard_map/ppermute | solution.py:16
  233.7 3.2 collective-permute-start.5
  237.0 4.1 %collective-permute-start.6 = (bf16[160,128]{0,1:T(8,128)(2,1)S(1)}, bf16[160,128]{0,1:T(8,128)(2,1)S(1)}, u32[]{:S(2)}, u32[]{:S(2)}) collective-permute-start(bf16[160,128]{0,1:T(8,128)(2,1)S(1)} %maximum_select_fusion.3), channel_id=1, source_target_pairs={{0,4},{4,0},{1,5},{5,1},{2,6},{6,2},{3,7},{7,3},{8,12},{12,8},{9,1... | collective-permute-start | bytes 122888 | tf_op jit(solution)/shard_map/ppermute | solution.py:16
Sparse Core Ops, SparseCore 0:
  9.2 37.3 all-gather.4
  48.5 35.2 all-gather.6
  88.1 68.0 all-reduce.1
  157.9 87.4 all-gather.8
  247.0 35.2 all-gather.10
  286.7 34.9 reduce-scatter.1
where the time goes:
time: 334 us; the launch traced here: 330 us
  waiting for transfers between devices  201 us (60%)
  blocking collectives  76.7 us (23%)
  matrix products  15.7 us (5%)
  starting transfers between devices  13.8 us (4%)
  between operations  13.6 us (4%)
  other arithmetic  9.28 us (3%)
    all_gather x2, blocking collectives, head_terms(): lax.all_gather(keyval_shard, 'inst', axis=0, tiled=True)  76.7 us
    all_gather x2, waiting for transfers between devices, head_terms(): lax.all_gather(output_shard, 'inst', axis=1, tiled=True)  68.8 us
    psum x1, waiting for transfers between devices, shards(): lax.psum(first_terms.astype(jnp.bfloat16), 'tp').astype(jnp.float32)  67.5 us
    reduce_scatter x1, waiting for transfers between devices, shards(): lax.psum_scatter(second_terms.astype(jnp.bfloat16), 'tp', scatter_dimensi...  35.1 us
    all_gather x2, waiting for transfers between devices, head_terms(): lax.all_gather(query_shard, 'inst', axis=0, tiled=True)  19.1 us
    ppermute x6, starting transfers between devices, from_partner(): return lax.ppermute(block, axis, route)  12.4 us
    ppermute x6, waiting for transfers between devices, from_partner(): return lax.ppermute(block, axis, route)  8.68 us
    dot_general x2, matrix products, head_terms(): jnp.dot(context, lax.all_gather(output_shard, 'inst', axis=1, tiled=True)...  8.31 us
  transfers between devices with their start and end apart: 13, of which 12 were waited for; matrix products, arithmetic and copies ran while one was open for 5% of the time, Pallas kernels for 0%

commit v1 on v0

v1 whole, which is shorter than its diff:
```python
import functools
import math

import jax
import jax.numpy as jnp
from jax import lax
from jax.experimental import pallas as pl
from jax.experimental.pallas import tpu as pltpu
from jax.sharding import PartitionSpec as P

GROUP = 8
EPS = 1e-6
LANES = 128
VMEM = pl.BlockSpec(memory_space=pltpu.VMEM)
HBM = pl.BlockSpec(memory_space=pltpu.MemorySpace.HBM)
LAST = pl.BlockSpec(memory_space=pltpu.VMEM)


def contract(left, right, dims):
    return lax.dot_general(left, right, ((dims[:1], dims[1:]), ((), ())), preferred_element_type=jnp.float32)


def after(value, *others):
    return lax.optimization_barrier((value, others))[0]


def exchange(block, axis, groups=None):
    return lax.all_to_all(block, axis, 0, 0, axis_index_groups=groups)


def other_core(block):
    count = lax.axis_size("tp")
    return lax.ppermute(block, "tp", [(s, s ^ 1) for s in range(count)])


def own_core():
    return lax.rem(lax.axis_index("tp"), 2)


def transposed(block, rows):
    row = lax.broadcasted_iota(jnp.int32, (rows, block.shape[1]), 0)
    column = lax.broadcasted_iota(jnp.int32, (rows, block.shape[1]), 1)
    pick = (row == column).astype(jnp.bfloat16)
    return contract(pick, block, (1, 1)).astype(jnp.bfloat16)


def call(kernel, name, outs, ins, args, scratch=(), places=None):
    places = places or [VMEM] * len(outs)
    held = [value for value, spec in zip([*args, *outs], [*ins, *places]) if spec is VMEM]
    total = sum(math.prod(value.shape) * value.dtype.itemsize for value in held)
    work = sum(math.prod(ref.shape) * ref.dtype.itemsize for ref in scratch if hasattr(ref.dtype, "itemsize"))
    resident = total <= 16 * 2**20
    if resident:
        spaces = [spec.memory_space for spec in ins]
        args = [pltpu.with_memory_space_constraint(value, space) for value, space in zip(args, spaces)]
        outs = [out if spec is LAST else spec.memory_space(out.shape, out.dtype) for out, spec in zip(outs, places)]
        limit = work + 12 * 2**20
    else:
        limit = 56 * 2**20
    return pl.pallas_call(
        kernel,
        out_shape=outs,
        in_specs=ins,
        out_specs=[VMEM if spec is LAST else spec for spec in places],
        scratch_shapes=list(scratch),
        compiler_params=pltpu.CompilerParams(vmem_limit_bytes=limit),
        name=name,
    )(*args)


def bfloat(*shape):
    return jax.ShapeDtypeStruct(shape, jnp.bfloat16)


def shifted(block, axis, distance):
    count = lax.axis_size(axis)
    return lax.ppermute(block, axis, [(s, (s + distance) % count) for s in range(count)])


def core_groups():
    ranks = lax.axis_size("tp")
    return [list(range(core, ranks, 2)) for core in range(2)]


def cut_kernel(tokens, shard, output, keyval, sent, bound, held, sems):
    count, both, width = sent.shape
    head = output.shape[0]
    sub = shard.shape[0] // count
    half = both - sub
    start = pl.multiple_of(own_core() * half, half)
    copies = [
        pltpu.make_async_copy(output, held.at[pl.ds(0, head), :], sems.at[2, 0]),
        pltpu.make_async_copy(keyval, held.at[pl.ds(head, keyval.shape[0]), :], sems.at[2, 1]),
    ]
    for q in range(count):
        source = tokens.at[pl.ds(start, half), pl.ds(q * width, width)]
        copies.append(pltpu.make_async_copy(source, sent.at[q, pl.ds(0, half)], sems.at[0, q]))
        source = shard.at[pl.ds(q * sub, sub), :]
        copies.append(pltpu.make_async_copy(source, sent.at[q, pl.ds(half, sub)], sems.at[1, q]))
    for copy in copies:
        copy.start()
    for copy in copies[:2]:
        copy.wait()
    save = pltpu.make_async_copy(held, bound, sems.at[2, 2])
    save.start()
    for copy in copies[2:]:
        copy.wait()
    save.wait()


def cut(tokens, shard, output, keyval, count):
    rows, depth = tokens.shape
    together = (output.shape[0] + keyval.shape[0], output.shape[1])
    outs = [bfloat(count, rows // 2 + shard.shape[0] // count, depth // count), bfloat(*together)]
    scratch = [pltpu.VMEM(together, jnp.bfloat16), pltpu.SemaphoreType.DMA((3, max(3, count)))]
    return call(cut_kernel, "cut", outs, [HBM] * 4, [tokens, shard, output, keyval], scratch, [VMEM, HBM])


def norm_kernel(tokens, scale, whole, sems):
    pieces = sems.shape[0]
    step = tokens.shape[1] // pieces
    copies = []
    for p in range(pieces):
        columns = pl.ds(p * step, step)
        copies.append(pltpu.make_async_copy(tokens.at[:, columns], whole.at[:, columns], sems.at[p]))
    for copy in copies:
        copy.start()
    total = jnp.zeros((tokens.shape[0], LANES), jnp.float32)
    for p, copy in enumerate(copies):
        copy.wait()
        for low in range(p * step, (p + 1) * step, LANES):
            floats = whole[:, low : low + LANES].astype(jnp.float32)
            total = total + floats * floats
    squares = jnp.sum(total, axis=1, keepdims=True)
    scale[...] = lax.rsqrt(squares / tokens.shape[1] + EPS)


def norms(tokens):
    outs = [jax.ShapeDtypeStruct((tokens.shape[0], 1), jnp.float32)]
    scratch = [pltpu.VMEM(tokens.shape, jnp.bfloat16), pltpu.SemaphoreType.DMA((4,))]
    return call(norm_kernel, "norms", outs, [HBM], [tokens], scratch)[0]


def part_kernel(got, mine):
    for q in range(mine.shape[0]):
        mine[q] = got[q, : mine.shape[1], :]


def part(got, half):
    return call(part_kernel, "part", [bfloat(got.shape[0], half, got.shape[2])], [VMEM], [got])[0]


def aim_kernel(got, heads, *pieces):
    planes = len(pieces)
    for e, piece in enumerate(pieces):
        half = got.shape[1] - piece.shape[0]
        piece[...] = got[lax.rem(lax.axis_index("tp") // 2 + e, planes), half:, :]


def aim(got, half, heads):
    planes = heads.shape[0]
    outs = [bfloat(got.shape[1] - half, got.shape[2])] * planes
    return call(aim_kernel, "aim", outs, [VMEM, VMEM], [got, heads])


def keep_kernel(source, output, *refs):
    pieces, (kept, rows) = refs[:-2], refs[-2:]
    kept[...] = source[...]
    for e, piece in enumerate(pieces):
        rows[e] = piece[...]


def keep(block, output, pieces):
    outs = [bfloat(*block.shape), bfloat(len(pieces), *pieces[0].shape)]
    ins = [VMEM, HBM] + [VMEM] * len(pieces)
    return call(keep_kernel, "keep", outs, ins, [block, output, *pieces], places=[VMEM, LAST])


def fill_tall(keyval, tall):
    piece = keyval.shape[0]
    tall[:piece, :] = keyval[...]
    tall[piece:, :] = jnp.zeros((LANES - piece, tall.shape[1]), tall.dtype)


def project_kernel(mine, other, query, keyval, saved, sums, held, tall, sem):
    count, half, _ = mine.shape
    core = own_core()
    for q in range(count):
        for source, place in ((mine, core), (other, 1 - core)):
            held[pl.ds(pl.multiple_of((2 * q + place) * half, half), half), :] = source[q]
    save = pltpu.make_async_copy(held, saved, sem)
    save.start()
    fill_tall(keyval, tall)
    hidden = held[...]
    head = query.shape[1]
    queries = jnp.dot(hidden, query[...], preferred_element_type=jnp.float32).astype(jnp.bfloat16)
    products = contract(hidden, tall[...], (1, 1)).astype(jnp.bfloat16)
    for q in range(count):
        sums[q, :, :head] = queries[2 * q * half : 2 * (q + 1) * half]
        sums[q, :, head:] = products[2 * q * half : 2 * (q + 1) * half]
    save.wait()


def project(mine, other, query, keyval):
    count, half, width = mine.shape
    rows = 2 * half
    outs = [bfloat(count * rows, width), bfloat(count, rows, query.shape[1] + LANES)]
    scratch = [
        pltpu.VMEM((count * rows, width), jnp.bfloat16),
        pltpu.VMEM((LANES, width), jnp.bfloat16),
        pltpu.SemaphoreType.DMA(()),
    ]
    args = [mine, other, query, keyval]
    return call(project_kernel, "project", outs, [VMEM] * 4, args, scratch, [HBM, VMEM])


def summed(parts):
    total = parts[0].astype(jnp.float32)
    for part in parts[1:]:
        total = total + part.astype(jnp.float32)
    return total


def finish_kernel(parts, scale, queries, keyvals_t):
    head = queries.shape[1]
    total = summed([parts[q] for q in range(parts.shape[0])]) * scale[...]
    queries[...] = (total[:, :head] * head ** (-0.5)).astype(jnp.bfloat16)
    piece = transposed(total[:, head:].astype(jnp.bfloat16), keyvals_t.shape[1])
    for g in range(keyvals_t.shape[0]):
        keyvals_t[g] = piece


def finish(parts, scale, head, piece):
    rows = parts.shape[1]
    outs = [bfloat(rows, head), bfloat(GROUP, piece, rows)]
    return call(finish_kernel, "finish", outs, [VMEM] * 2, [parts, scale])


def attention(queries, keys_t, values_t, dims, doc_ids, back):
    rows = queries.shape[0]
    at = lax.broadcasted_iota(jnp.int32, (rows, rows), 0)
    key_at = lax.broadcasted_iota(jnp.int32, (rows, rows), 1)
    count = doc_ids.shape[0]
    own = lax.rem(lax.axis_index("inst") - back + count, count)
    docs_row = jnp.broadcast_to(doc_ids[pl.ds(own, 1), :].astype(jnp.float32), (rows, rows))
    docs_column = jnp.sum(jnp.where(at == key_at, docs_row, 0.0), axis=1, keepdims=True)
    allowed = (docs_column == docs_row) & (key_at <= at)
    scores = contract(queries, keys_t, (1, dims[0]))
    scores = jnp.where(allowed, scores, -1e30)
    weights = jnp.exp(scores - jnp.max(scores, axis=1, keepdims=True))
    probabilities = weights / jnp.sum(weights, axis=1, keepdims=True)
    return contract(probabilities.astype(jnp.bfloat16), values_t, (1, dims[1])).astype(jnp.bfloat16)


def first_kernel(queries, doc_ids, pieces, context):
    span = pieces.shape[0] // 2
    keys_t = jnp.concatenate([pieces[g] for g in range(span)], 0)
    values_t = jnp.concatenate([pieces[g] for g in range(span, 2 * span)], 0)
    result = attention(queries[...], keys_t, values_t, (0, 1), doc_ids, 0)
    for z in range(context.shape[0]):
        context[z] = result


def first_attend(queries, doc_ids, pieces):
    outs = [bfloat(lax.axis_size("tp") // 2, *queries.shape)]
    return call(first_kernel, "attend", outs, [VMEM] * 3, [queries, doc_ids, pieces])[0]


def second_kernel(depth, head, rows, parts, doc_ids, sent):
    wide = 3 * head
    total = summed([parts[q, :rows, :wide] for q in range(parts.shape[0])])
    high = summed([parts[q, rows : rows + 16, :] for q in range(parts.shape[0])])
    across = jnp.broadcast_to(high[0:1] + high[1:2], (rows, parts.shape[2]))
    at = lax.broadcasted_iota(jnp.int32, across.shape, 0)
    lane = lax.broadcasted_iota(jnp.int32, across.shape, 1)
    squares = jnp.sum(jnp.where(at == lane, across, 0.0), axis=1, keepdims=True)
    total = total * lax.rsqrt(squares / depth + EPS)
    queries = (total[:, :head] * head ** (-0.5)).astype(jnp.bfloat16)
    keys = total[:, head : 2 * head].astype(jnp.bfloat16)
    values = total[:, 2 * head :].astype(jnp.bfloat16)
    result = attention(queries, keys, values, (1, 0), doc_ids, 1)
    for z in range(sent.shape[0]):
        sent[z, :, :head] = result
        sent[z, :, head:] = parts[z, :rows, wide:]


def second_attend(parts, doc_ids, depth, head):
    rows = doc_ids.shape[1]
    outs = [bfloat(parts.shape[0], rows, parts.shape[2] - 2 * head)]
    kernel = functools.partial(second_kernel, depth, head, rows)
    return call(kernel, "attend", outs, [VMEM] * 2, [parts, doc_ids])[0]


def spread_kernel(heads, sent):
    for q in range(sent.shape[0]):
        sent[q] = heads[...]


def spread(heads):
    outs = [bfloat(lax.axis_size("inst"), *heads.shape)]
    return call(spread_kernel, "spread", outs, [VMEM], [heads])[0]


def spans(count):
    return [range(low, min(low + 4, count)) for low in range(0, count, 4)]


def place_contexts(mine, other, left, span):
    _, pairs, rows, head = mine.shape
    core = own_core()
    for source, parity in ((mine, core), (other, 1 - core)):
        for e in range(pairs):
            columns = pl.ds(pl.multiple_of((2 * e + parity) * head, head), head)
            for at, q in enumerate(span):
                left[at * rows : (at + 1) * rows, columns] = source[q, e]


def advance_kernel(step, before, mine, other, output, query, sums, left, held, tall, hidden, blended, sems):
    count, pairs, rows, head = mine.shape
    width = before.shape[1]
    ranks = 2 * pairs
    first = lax.axis_index("tp") // GROUP * GROUP
    copies = []
    for at in range(width // step):
        columns = pl.ds(at * step, step)
        pairs_of = [
            (output.at[:, pl.ds(0, head), columns], held.at[:, :, columns]),
            (before.at[:, columns], hidden.at[:, columns]),
            (output.at[pl.ds(first, GROUP), pl.ds(head, tall.shape[1]), columns], tall.at[:, :, columns]),
        ]
        copies.append([pltpu.make_async_copy(*pair, sems.at[c, at]) for c, pair in enumerate(pairs_of)])
    for chunk in copies:
        for copy in chunk:
            copy.start()
    for span in spans(count):
        place_contexts(mine, other, left, span)
        low, high = span[0] * rows, (span[-1] + 1) * rows
        queries, keyvals, squares = 0.0, 0.0, 0.0
        for at, chunk in enumerate(copies):
            if span[0] == 0:
                for copy in chunk:
                    copy.wait()
            columns = pl.ds(at * step, step)
            right = held[:, :, columns].reshape(ranks * head, step)
            attended = jnp.dot(left[: high - low, :], right, preferred_element_type=jnp.float32)
            after_one = (hidden[low:high, columns].astype(jnp.float32) + attended).astype(jnp.bfloat16)
            blended[low:high, columns] = after_one
            queries = queries + jnp.dot(after_one, query[columns, :], preferred_element_type=jnp.float32)
            right = tall[:, :, columns].reshape(GROUP * tall.shape[1], step)
            keyvals = keyvals + contract(after_one, right, (1, 1))
            floats = after_one.astype(jnp.float32)
            squares = squares + jnp.sum(floats * floats, axis=1, keepdims=True)
        queries, keyvals = queries.astype(jnp.bfloat16), keyvals.astype(jnp.bfloat16)
        for at, q in enumerate(span):
            slot = (q + 1) % count
            block = slice(at * rows, (at + 1) * rows)
            sums[slot, :rows, :head] = queries[block]
            sums[slot, :rows, head : 3 * head] = keyvals[block]
            lanes = sums.shape[2]
            row = lax.broadcasted_iota(jnp.int32, (rows, lanes), 0)
            lane = lax.broadcasted_iota(jnp.int32, (rows, lanes), 1)
            square = jnp.where(row == lane, squares[block], 0.0)
            square = jnp.sum(square, axis=0, keepdims=True)
            high_part = square.astype(jnp.bfloat16).astype(jnp.float32)
            row = lax.broadcasted_iota(jnp.int32, (16, lanes), 0)
            extra = jnp.where(row == 0, high_part, jnp.where(row == 1, square - high_part, 0.0))
            sums[slot, rows:, :] = extra.astype(jnp.bfloat16)
    wide = 3 * head
    slim = (sums.shape[2] - wide) // 2
    for r in range(ranks):

        @pl.when(lax.axis_index("tp") == r)
        def give():
            for b in range(2):
                low = b * (width // 2) + r * slim
                for q in range(count):
                    block = blended[q * rows : (q + 1) * rows, low : low + slim]
                    sums[(q + 1) % count, :rows, wide + b * slim : wide + (b + 1) * slim] = block


def advance(before, mine, other, output, query):
    count, pairs, rows, head = mine.shape
    total, width = before.shape
    step = min(512, width)
    ranks, both, _ = output.shape
    scratch = [
        pltpu.VMEM((min(4, count) * rows, ranks * head), jnp.bfloat16),
        pltpu.VMEM((ranks, head, width), jnp.bfloat16),
        pltpu.VMEM((GROUP, both - head, width), jnp.bfloat16),
        pltpu.VMEM((total, width), jnp.bfloat16),
        pltpu.VMEM((total, width), jnp.bfloat16),
        pltpu.SemaphoreType.DMA((3, width // step)),
    ]
    outs = [bfloat(count, rows + 16, 3 * head + width // ranks)]
    ins = [HBM] + [VMEM] * 2 + [HBM, VMEM]
    args = [before, mine, other, output, query]
    return call(functools.partial(advance_kernel, step), "advance", outs, ins, args, scratch)[0]


def blend_kernel(got, rows_by, kept, sent, held, sems):
    pairs, rows, _ = got.shape
    count, _, sub, _ = rows_by.shape
    head = count * sub
    plane = lax.axis_index("tp") // 2
    copies = []
    for i in range(count):
        for e in range(pairs):
            target = held.at[pl.ds(e * head + i * sub, sub), :]
            copies.append(pltpu.make_async_copy(rows_by.at[i, e], target, sems.at[i, e]))
    for copy in copies:
        copy.start()
    left = jnp.concatenate([got[lax.rem(plane - e + pairs, pairs), :, :head] for e in range(pairs)], 1)
    half = kept.shape[1]
    slim = half // (2 * pairs)
    for copy in copies:
        copy.wait()
    for core in range(2):

        @pl.when(own_core() == core)
        def give():
            for b in range(2):
                rest = []
                for a in range(pairs):
                    ours = got[a, :, head + b * slim : head + (b + 1) * slim]
                    rest += [ours, jnp.zeros_like(ours)] if core == 0 else [jnp.zeros_like(ours), ours]
                rest = jnp.concatenate(rest, 1).astype(jnp.float32)
                right = held[:, b * half : (b + 1) * half]
                total = jnp.dot(left, right, preferred_element_type=jnp.float32) + rest
                if b == core:
                    kept[...] = total
                else:
                    sent[...] = total.astype(jnp.bfloat16)


def blend(got, rows_by):
    pairs, rows, _ = got.shape
    count, _, sub, width = rows_by.shape
    scratch = [pltpu.VMEM((pairs * count * sub, width), jnp.bfloat16), pltpu.SemaphoreType.DMA((count, pairs))]
    outs = [jax.ShapeDtypeStruct((rows, width // 2), jnp.float32), bfloat(rows, width // 2)]
    return call(blend_kernel, "blend", outs, [VMEM, HBM], [got, rows_by], scratch)


def join_kernel(kept, arrived, blended):
    blended[...] = (kept[...] + arrived[...].astype(jnp.float32)).astype(jnp.bfloat16)


def join(kept, arrived):
    return call(join_kernel, "join", [bfloat(*kept.shape)], [VMEM] * 2, [kept, arrived], places=[LAST])[0]


def shards(tokens, doc_ids, query_one, keyval_one, output_one, query_two, keyval_two, output_two):
    count, ranks = lax.axis_size("inst"), lax.axis_size("tp")
    rows, depth = tokens.shape
    head, piece = query_one.shape[1], keyval_one.shape[1]
    groups = None
    if ranks > GROUP:
        groups = [list(range(low, low + GROUP)) for low in range(0, ranks, GROUP)]

    sent, bound = cut(tokens, output_two, output_one, keyval_two.T, count)
    output_all = lax.all_gather(bound, "tp", axis=0)
    got = exchange(sent, "inst")
    mine = part(got, rows // 2)
    held, sums = project(mine, other_core(mine), query_one, keyval_one.T)
    queries, keyvals_t = finish(exchange(sums, "inst"), norms(tokens), head, piece)
    context = first_attend(queries, doc_ids, exchange(keyvals_t, "tp", groups))
    heads = exchange(context, "tp", core_groups())
    pieces = aim(got, rows // 2, heads)
    pieces = [pieces[0]] + [shifted(pieces[e], "tp", 2 * e) for e in range(1, ranks // 2)]
    mine, rows_by = keep(exchange(spread(heads), "inst"), output_all, pieces)
    rows_by = lax.all_gather(rows_by, "inst", axis=0)
    sums = advance(held, mine, other_core(mine), output_all, query_two)

    sent = second_attend(exchange(sums, "inst"), doc_ids, depth, head)
    kept, sent = blend(exchange(sent, "tp", core_groups()), rows_by)
    return join(kept, other_core(sent))


def solution(mesh):
    placed = (
        P("inst", None),
        P(),
        P("inst", "tp"),
        P("inst", "tp"),
        P("tp", "inst"),
        P("inst", "tp"),
        P("inst", "tp"),
        P("tp", "inst"),
    )
    return jax.shard_map(
        shards, mesh=mesh, in_specs=placed, out_specs=P("inst", "tp"), check_vma=False
    )
```

time: 334 us -> 154 us (0.46)
  waiting for transfers between devices: 201 us -> 17.7 us
  Pallas kernels: 0 us -> 20.6 us
  matrix products: 15.7 us -> 0 us
  other arithmetic: 9.28 us -> 0 us
  blocking collectives: 76.7 us -> 84.1 us
    all_gather x4 -> x2, waiting for transfers between devices: 87.9 us -> 0.01 us  [the longest x1 0.01 us: shards(): output_all = lax.all_gather(bound, 'tp', axis=0)]
    all_to_all x0 -> x5, blocking collectives: none -> 84.1 us  [exchange(): return lax.all_to_all(block, axis, 0, 0, axis_index_groups=groups)]
    all_gather x2 -> x0, blocking collectives: 76.7 us -> none  [head_terms(): lax.all_gather(keyval_shard, 'inst', axis=0, tiled=True)]
    psum x1 -> x0, waiting for transfers between devices: 67.5 us -> none  [shards(): lax.psum(first_terms.astype(jnp.bfloat16), 'tp').astype(jnp.float32)]
    reduce_scatter x1 -> x0, waiting for transfers between devices: 35.1 us -> none  [shards(): lax.psum_scatter(second_terms.astype(jnp.bfloat16), 'tp', scatter_dimensi...]
    pallas_call x0 -> x13, Pallas kernels: none -> 20.6 us  [call(): pl.pallas_call(kernel, out_shape=outs, in_specs=ins, out_specs=[VMEM if s...]
    dot_general x6 -> x0, matrix products: 15.7 us -> none  [the longest x2 8.31 us: head_terms(): jnp.dot(context, lax.all_gather(output_shard, 'inst', axis=1, tiled=True)...]
    all_to_all x0 -> x2, starting transfers between devices: none -> 6.95 us  [exchange(): return lax.all_to_all(block, axis, 0, 0, axis_index_groups=groups)]
  transfers between devices with their start and end apart: 13 -> 10, of which waited for: 12 -> 6; matrix products, arithmetic and copies ran while one was open for 5% -> 0% of each run, Pallas kernels for 0% -> 9%
where the time goes in v1:
time: 154 us
  blocking collectives  84.1 us (55%)
  Pallas kernels  20.6 us (13%)
  waiting for transfers between devices  17.7 us (11%)
  starting transfers between devices  16.4 us (11%)
  between operations  13.5 us (9%)
    all_to_all x5, blocking collectives, exchange(): return lax.all_to_all(block, axis, 0, 0, axis_index_groups=groups)  84.1 us
    pallas_call x13, Pallas kernels, call(): pl.pallas_call(kernel, out_shape=outs, in_specs=ins, out_specs=[VMEM if s...  20.6 us
    ppermute x3, waiting for transfers between devices, shifted(): lax.ppermute(block, axis, [(s, (s + distance) % count) for s in range(cou...  8.28 us
    all_to_all x2, starting transfers between devices, exchange(): return lax.all_to_all(block, axis, 0, 0, axis_index_groups=groups)  6.95 us
    ppermute x3, waiting for transfers between devices, other_core(): return lax.ppermute(block, 'tp', [(s, s ^ 1) for s in range(count)])  5.64 us
    ppermute x3, starting transfers between devices, other_core(): return lax.ppermute(block, 'tp', [(s, s ^ 1) for s in range(count)])  5.56 us
    ppermute x3, starting transfers between devices, shifted(): lax.ppermute(block, axis, [(s, (s + distance) % count) for s in range(cou...  3.8 us
    all_to_all x2, waiting for transfers between devices, exchange(): return lax.all_to_all(block, axis, 0, 0, axis_index_groups=groups)  3.77 us
  transfers between devices with their start and end apart: 10, of which 6 were waited for; matrix products, arithmetic and copies ran while one was open for 0% of the time, Pallas kernels for 9%

profile of v1, /device:TPU:1, one launch (start us, length us, event | category | flops | bytes accessed | tf_op | source)
XLA Modules:
  0.0 153.6 jit_solution(13806381259423810736)
XLA Ops:
  6.5 0.0 all-gather.5.cloned.1.call-start
  6.5 2.1 %cut.1 = (bf16[4,112,2048]{2,1,0:T(8,128)(2,1)S(1)}, bf16[160,2048]{1,0:T(8,128)(2,1)}) custom-call(bf16[160,8192]{1,0:T(8,128)(2,1)} %tokens.3, bf16[128,2048]{1,0:T(8,128)(2,1)} %shard.1, bf16[128,2048]{1,0:T(8,128)(2,1)} %output.1, bf16[32,2048]{1,0:T(8,128)(2,1)} %bitcast.8), custom_call_target="tpu_custom_call" | custom-call | tf_op jit(solution)/shard_map/cut/pallas_call | solution.py:60
  8.6 0.0 copy-start
  8.6 1.2 copy-done
  9.9 0.0 all-gather.5.cloned.1.call-update
  9.9 25.7 %all_to_all.35.got = bf16[4,112,2048]{2,1,0:T(8,128)(2,1)S(1)} all-to-all(bf16[4,112,2048]{2,1,0:T(8,128)(2,1)} %copy-done), channel_id=1, replica_groups=mesh['inst'=4,'tp'=8] {'inst'}, dimensions={0} | all-to-all | bytes 3670016 | tf_op jit(solution)/shard_map/all_to_all | solution.py:28
  35.5 0.0 copy-start.1
  35.5 0.0 copy-start.3
  35.5 0.1 part.1.mine
  35.6 2.2 %collective-permute-start = (bf16[4,80,2048]{2,1,0:T(8,128)(2,1)S(1)}, bf16[4,80,2048]{2,1,0:T(8,128)(2,1)S(1)}, u32[]{:S(2)}, u32[]{:S(2)}) collective-permute-start(bf16[4,80,2048]{2,1,0:T(8,128)(2,1)S(1)} %part.1.mine), channel_id=1, source_target_pairs={{0,1},{1,0},{2,3},{3,2},{4,5},{5,4},{6,7},{7,6},{8,9},{9,8},{10,11... | collective-permute-start | bytes 3932168 | tf_op jit(solution)/shard_map/ppermute | solution.py:33
  37.8 2.7 %collective-permute-done.other = bf16[4,80,2048]{2,1,0:T(8,128)(2,1)S(1)} collective-permute-done((bf16[4,80,2048]{2,1,0:T(8,128)(2,1)S(1)}, bf16[4,80,2048]{2,1,0:T(8,128)(2,1)S(1)}, u32[]{:S(2)}, u32[]{:S(2)}) %collective-permute-start) | collective-permute-done | bytes 1310752 | tf_op jit(solution)/shard_map/ppermute | solution.py:33
  40.5 0.0 copy-done.1
  40.5 0.0 copy-done.3
  40.5 3.6 %project.1 = (bf16[640,2048]{1,0:T(8,128)(2,1)}, bf16[4,160,256]{2,1,0:T(8,128)(2,1)}) custom-call(bf16[4,80,2048]{2,1,0:T(8,128)(2,1)S(1)} %part.1.mine, bf16[4,80,2048]{2,1,0:T(8,128)(2,1)S(1)} %collective-permute-done.other, bf16[2048,128]{1,0:T(8,128)(2,1)S(1)} %copy-done.1, bf16[32,2048]{1,0:T(8,128)(2,1)S(1)} %bitcast.4), custom_call_target="tpu_custom_call" | custom-call | tf_op jit(solution)/shard_map/project/pallas_call | solution.py:60
  44.1 0.0 copy-start.4
  44.1 3.5 %all-to-all-start.1 = ((bf16[4,160,256]{2,1,0:T(8,128)(2,1)}), bf16[4,160,256]{2,1,0:T(8,128)(2,1)S(1)}, u32[]{:S(2)}, u32[]{:S(2)}) async-start(bf16[4,160,256]{2,1,0:T(8,128)(2,1)} %get-tuple-element.21), calls=%async_computation.1 | async-start | bytes 655360 | tf_op jit(solution)/shard_map/all_to_all | solution.py:28
  47.6 1.9 %norms.1.scale = f32[160,1]{1,0:T(8,128)S(1)} custom-call(bf16[160,8192]{1,0:T(8,128)(2,1)} %tokens.3), custom_call_target="tpu_custom_call" | custom-call | tf_op jit(solution)/shard_map/norms/pallas_call | solution.py:60
  49.5 3.8 %all-to-all-done.1.parts = bf16[4,160,256]{2,1,0:T(8,128)(2,1)S(1)} async-done(((bf16[4,160,256]{2,1,0:T(8,128)(2,1)}), bf16[4,160,256]{2,1,0:T(8,128)(2,1)S(1)}, u32[]{:S(2)}, u32[]{:S(2)}) %all-to-all-start.1) | async-done | bytes 327712 | tf_op jit(solution)/shard_map/all_to_all | solution.py:28
  53.3 0.2 finish.1
  53.5 15.5 %all_to_all.36.pieces = bf16[8,32,160]{2,1,0:T(8,128)(2,1)S(1)} all-to-all(bf16[8,32,160]{2,1,0:T(8,128)(2,1)S(1)} %get-tuple-element.23), channel_id=1, replica_groups=mesh['inst'=4,'tp'=8] {'tp'}, dimensions={0} | all-to-all | bytes 163840 | tf_op jit(solution)/shard_map/all_to_all | solution.py:28
  69.1 0.0 copy-done.4
  69.1 0.5 attend.2
  69.5 7.9 %all_to_all.37.heads = bf16[4,160,128]{2,1,0:T(8,128)(2,1)S(1)} all-to-all(bf16[4,160,128]{2,1,0:T(8,128)(2,1)S(1)} %attend.2), channel_id=1, replica_groups={{0,2,4,6},{1,3,5,7},{8,10,12,14},{9,11,13,15},{16,18,20,22},{17,19,21,2..., dimensions={0} | all-to-all | bytes 327680 | tf_op jit(solution)/shard_map/all_to_all | solution.py:28
  77.5 1.0 spread.1
  78.4 3.5 %all-to-all-start.4 = ((bf16[4,4,160,128]{3,2,1,0:T(8,128)(2,1)}), bf16[4,4,160,128]{3,2,1,0:T(8,128)(2,1)S(1)}, u32[]{:S(2)}, u32[]{:S(2)}) async-start(bf16[4,4,160,128]{3,2,1,0:T(8,128)(2,1)} %spread.1), calls=%async_computation.4 | async-start | bytes 1310720 | tf_op jit(solution)/shard_map/all_to_all | solution.py:28
  81.9 0.0 all-gather.7.cloned.1.call-start
  82.0 0.1 aim.1
  82.0 0.6 collective-permute-start.1
  82.6 2.2 %collective-permute-start.2 = (bf16[32,2048]{1,0:T(8,128)(2,1)S(1)}, bf16[32,2048]{1,0:T(8,128)(2,1)S(1)}, u32[]{:S(2)}, u32[]{:S(2)}) collective-permute-start(bf16[32,2048]{1,0:T(8,128)(2,1)S(1)} %get-tuple-element.27), channel_id=1, source_target_pairs={{0,4},{1,5},{2,6},{3,7},{4,0},{5,1},{6,2},{7,3},{8,12},{9,13},{10,... | collective-permute-start | bytes 393224 | tf_op jit(solution)/shard_map/ppermute | solution.py:77
  84.8 1.0 collective-permute-start.3
  85.8 2.0 %collective-permute-done.1.refs_1_ = bf16[32,2048]{1,0:T(8,128)(2,1)S(1)} collective-permute-done((bf16[32,2048]{1,0:T(8,128)(2,1)S(1)}, bf16[32,2048]{1,0:T(8,128)(2,1)S(1)}, u32[]{:S(2)}, u32[]{:S(2)}) %collective-permute-start.1) | collective-permute-done | bytes 131104 | tf_op jit(solution)/shard_map/ppermute | solution.py:77
  87.9 6.2 %collective-permute-done.2.refs_2_ = bf16[32,2048]{1,0:T(8,128)(2,1)S(1)} collective-permute-done((bf16[32,2048]{1,0:T(8,128)(2,1)S(1)}, bf16[32,2048]{1,0:T(8,128)(2,1)S(1)}, u32[]{:S(2)}, u32[]{:S(2)}) %collective-permute-start.2) | collective-permute-done | bytes 131104 | tf_op jit(solution)/shard_map/ppermute | solution.py:77
  94.1 0.0 collective-permute-done.3.refs_3_
  94.1 0.0 all-to-all-done.4.source
  94.1 0.0 all-gather.5.cloned.1.call-done
  94.2 0.0 copy-start.2
  94.2 0.9 keep.1
  95.1 0.0 all-gather.7.cloned.1.call-update
  95.1 1.6 %collective-permute-start.4 = (bf16[4,4,160,128]{3,2,1,0:T(8,128)(2,1)S(1)}, bf16[4,4,160,128]{3,2,1,0:T(8,128)(2,1)S(1)}, u32[]{:S(2)}, u32[]{:S(2)}) collective-permute-start(bf16[4,4,160,128]{3,2,1,0:T(8,128)(2,1)S(1)} %get-tuple-element.29.mine), channel_id=1, source_target_pairs={{0,1},{1,0},{2,3},{3,2},{4,5},{5,4},{6,7},{7,6},{8,9},{9,8},{10,11... | collective-permute-start | bytes 1966088 | tf_op jit(solution)/shard_map/ppermute | solution.py:33
  96.7 1.7 %collective-permute-done.4.other = bf16[4,4,160,128]{3,2,1,0:T(8,128)(2,1)S(1)} collective-permute-done((bf16[4,4,160,128]{3,2,1,0:T(8,128)(2,1)S(1)}, bf16[4,4,160,128]{3,2,1,0:T(8,128)(2,1)S(1)}, u32[]{:S(2)}, u32[]{:S(2)}) %collective-permute-start.4) | collective-permute-done | bytes 655392 | tf_op jit(solution)/shard_map/ppermute | solution.py:33
  98.4 0.0 copy-done.2
  98.4 6.7 %advance.1 = bf16[4,176,640]{2,1,0:T(8,128)(2,1)S(1)} custom-call(bf16[640,2048]{1,0:T(8,128)(2,1)} %get-tuple-element.20.before, bf16[4,4,160,128]{3,2,1,0:T(8,128)(2,1)S(1)} %get-tuple-element.29.mine, bf16[4,4,160,128]{3,2,1,0:T(8,128)(2,1)S(1)} %collective-permute-done.4.other, bf16[8,160,2048]{2,1,0:T(8,128)(2,1)} %bitcast.6, ...), custom_call_target="tpu_custom_call" | custom-call | tf_op jit(solution)/shard_map/advance/pallas_call | solution.py:60
  105.1 17.8 %all_to_all.38.parts = bf16[4,176,640]{2,1,0:T(8,128)(2,1)S(1)} all-to-all(bf16[4,176,640]{2,1,0:T(8,128)(2,1)S(1)} %advance.1), channel_id=1, replica_groups=mesh['inst'=4,'tp'=8] {'inst'}, dimensions={0} | all-to-all | bytes 1802240 | tf_op jit(solution)/shard_map/all_to_all | solution.py:28
  122.9 0.6 attend.3
  123.5 17.2 %all_to_all.39.got = bf16[4,160,384]{2,1,0:T(8,128)(2,1)S(1)} all-to-all(bf16[4,160,384]{2,1,0:T(8,128)(2,1)S(1)} %attend.3), channel_id=1, replica_groups={{0,2,4,6},{1,3,5,7},{8,10,12,14},{9,11,13,15},{16,18,20,22},{17,19,21,2..., dimensions={0} | all-to-all | bytes 983040 | tf_op jit(solution)/shard_map/all_to_all | solution.py:28
  140.7 0.0 all-gather.7.cloned.1.call-done
  140.7 2.2 %blend.1 = (f32[160,1024]{1,0:T(8,128)S(1)}, bf16[160,1024]{1,0:T(8,128)(2,1)S(1)}) custom-call(bf16[4,160,384]{2,1,0:T(8,128)(2,1)S(1)} %all_to_all.39.got, bf16[4,4,32,2048]{3,2,1,0:T(8,128)(2,1)} %bitcast.7), custom_call_target="tpu_custom_call" | custom-call | tf_op jit(solution)/shard_map/blend/pallas_call | solution.py:60
  142.9 1.8 %collective-permute-start.5 = (bf16[160,1024]{1,0:T(8,128)(2,1)S(1)}, bf16[160,1024]{1,0:T(8,128)(2,1)S(1)}, u32[]{:S(2)}, u32[]{:S(2)}) collective-permute-start(bf16[160,1024]{1,0:T(8,128)(2,1)S(1)} %get-tuple-element.32), channel_id=1, source_target_pairs={{0,1},{1,0},{2,3},{3,2},{4,5},{5,4},{6,7},{7,6},{8,9},{9,8},{10,11... | collective-permute-start | bytes 983048 | tf_op jit(solution)/shard_map/ppermute | solution.py:33
  144.7 1.3 collective-permute-done.5.arrived
  145.9 0.8 join.1
Async XLA Ops:
  6.5 87.6 %all-gather.5.cloned.1.call-start = ((), (), s32[]{:S(2)}) async-start(), calls=%async_computation.7 | async-start | bytes 5898240 | tf_op jit(solution)/shard_map/all_gather | solution.py:460
  8.6 1.2 copy-start
  35.5 5.0 %copy-start.1 = (bf16[2048,128]{1,0:T(8,128)(2,1)S(1)}, bf16[2048,128]{1,0:T(8,128)(2,1)}, u32[]{:S(2)}) copy-start(bf16[2048,128]{1,0:T(8,128)(2,1)} %query.2) | copy-start | bytes 1572868
  35.5 5.0 %copy-start.3 = (bf16[2048,32]{0,1:T(8,128)(2,1)S(1)}, bf16[2048,32]{0,1:T(8,128)(2,1)}, u32[]{:S(2)}) copy-start(bf16[2048,32]{0,1:T(8,128)(2,1)} %param.11) | copy-start | bytes 393220
  35.6 4.9 %collective-permute-start = (bf16[4,80,2048]{2,1,0:T(8,128)(2,1)S(1)}, bf16[4,80,2048]{2,1,0:T(8,128)(2,1)S(1)}, u32[]{:S(2)}, u32[]{:S(2)}) collective-permute-start(bf16[4,80,2048]{2,1,0:T(8,128)(2,1)S(1)} %part.1.mine), channel_id=1, source_target_pairs={{0,1},{1,0},{2,3},{3,2},{4,5},{5,4},{6,7},{7,6},{8,9},{9,8},{10,11... | collective-permute-start | bytes 3932168 | tf_op jit(solution)/shard_map/ppermute | solution.py:33
  44.1 25.0 %copy-start.4 = (s32[4,160]{1,0:T(4,128)S(1)}, s32[4,160]{1,0:T(4,128)}, u32[]{:S(2)}) copy-start(s32[4,160]{1,0:T(4,128)} %doc_ids.3) | copy-start | bytes 7684
  44.1 9.2 %all-to-all-start.1 = ((bf16[4,160,256]{2,1,0:T(8,128)(2,1)}), bf16[4,160,256]{2,1,0:T(8,128)(2,1)S(1)}, u32[]{:S(2)}, u32[]{:S(2)}) async-start(bf16[4,160,256]{2,1,0:T(8,128)(2,1)} %get-tuple-element.21), calls=%async_computation.1 | async-start | bytes 655360 | tf_op jit(solution)/shard_map/all_to_all | solution.py:28
  78.4 15.7 %all-to-all-start.4 = ((bf16[4,4,160,128]{3,2,1,0:T(8,128)(2,1)}), bf16[4,4,160,128]{3,2,1,0:T(8,128)(2,1)S(1)}, u32[]{:S(2)}, u32[]{:S(2)}) async-start(bf16[4,4,160,128]{3,2,1,0:T(8,128)(2,1)} %spread.1), calls=%async_computation.4 | async-start | bytes 1310720 | tf_op jit(solution)/shard_map/all_to_all | solution.py:28
  81.9 58.7 %all-gather.7.cloned.1.call-start = ((), (), s32[]{:S(2)}) async-start(), calls=%async_computation.8 | async-start | bytes 2621440 | tf_op jit(solution)/shard_map/all_gather | solution.py:470
  82.0 5.8 %collective-permute-start.1 = (bf16[32,2048]{1,0:T(8,128)(2,1)S(1)}, bf16[32,2048]{1,0:T(8,128)(2,1)S(1)}, u32[]{:S(2)}, u32[]{:S(2)}) collective-permute-start(bf16[32,2048]{1,0:T(8,128)(2,1)S(1)} %get-tuple-element.26), channel_id=1, source_target_pairs={{0,2},{1,3},{2,4},{3,5},{4,6},{5,7},{6,0},{7,1},{8,10},{9,11},{10,... | collective-permute-start | bytes 393224 | tf_op jit(solution)/shard_map/ppermute | solution.py:77
  82.6 11.5 %collective-permute-start.2 = (bf16[32,2048]{1,0:T(8,128)(2,1)S(1)}, bf16[32,2048]{1,0:T(8,128)(2,1)S(1)}, u32[]{:S(2)}, u32[]{:S(2)}) collective-permute-start(bf16[32,2048]{1,0:T(8,128)(2,1)S(1)} %get-tuple-element.27), channel_id=1, source_target_pairs={{0,4},{1,5},{2,6},{3,7},{4,0},{5,1},{6,2},{7,3},{8,12},{9,13},{10,... | collective-permute-start | bytes 393224 | tf_op jit(solution)/shard_map/ppermute | solution.py:77
  84.8 9.3 %collective-permute-start.3 = (bf16[32,2048]{1,0:T(8,128)(2,1)S(1)}, bf16[32,2048]{1,0:T(8,128)(2,1)S(1)}, u32[]{:S(2)}, u32[]{:S(2)}) collective-permute-start(bf16[32,2048]{1,0:T(8,128)(2,1)S(1)} %get-tuple-element.28), channel_id=1, source_target_pairs={{0,6},{1,7},{2,0},{3,1},{4,2},{5,3},{6,4},{7,5},{8,14},{9,15},{10,... | collective-permute-start | bytes 393224 | tf_op jit(solution)/shard_map/ppermute | solution.py:77
  94.2 4.3 %copy-start.2 = (bf16[2048,128]{1,0:T(8,128)(2,1)S(1)}, bf16[2048,128]{1,0:T(8,128)(2,1)}, u32[]{:S(2)}) copy-start(bf16[2048,128]{1,0:T(8,128)(2,1)} %query.3) | copy-start | bytes 1572868
  95.1 3.3 %collective-permute-start.4 = (bf16[4,4,160,128]{3,2,1,0:T(8,128)(2,1)S(1)}, bf16[4,4,160,128]{3,2,1,0:T(8,128)(2,1)S(1)}, u32[]{:S(2)}, u32[]{:S(2)}) collective-permute-start(bf16[4,4,160,128]{3,2,1,0:T(8,128)(2,1)S(1)} %get-tuple-element.29.mine), channel_id=1, source_target_pairs={{0,1},{1,0},{2,3},{3,2},{4,5},{5,4},{6,7},{7,6},{8,9},{9,8},{10,11... | collective-permute-start | bytes 1966088 | tf_op jit(solution)/shard_map/ppermute | solution.py:33
  142.9 3.0 %collective-permute-start.5 = (bf16[160,1024]{1,0:T(8,128)(2,1)S(1)}, bf16[160,1024]{1,0:T(8,128)(2,1)S(1)}, u32[]{:S(2)}, u32[]{:S(2)}) collective-permute-start(bf16[160,1024]{1,0:T(8,128)(2,1)S(1)} %get-tuple-element.32), channel_id=1, source_target_pairs={{0,1},{1,0},{2,3},{3,2},{4,5},{5,4},{6,7},{7,6},{8,9},{9,8},{10,11... | collective-permute-start | bytes 983048 | tf_op jit(solution)/shard_map/ppermute | solution.py:33
Sparse Core Ops, SparseCore 0:
  10.0 61.4 all-gather.4
  95.2 42.7 all-gather.6

commit v2 on v1

--- a/solution.py
+++ b/solution.py
@@ -18,10 +18,6 @@
 
 def contract(left, right, dims):
     return lax.dot_general(left, right, ((dims[:1], dims[1:]), ((), ())), preferred_element_type=jnp.float32)
-
-
-def after(value, *others):
-    return lax.optimization_barrier((value, others))[0]
 
 
 def exchange(block, axis, groups=None):
@@ -82,38 +78,51 @@
     return [list(range(core, ranks, 2)) for core in range(2)]
 
 
-def cut_kernel(tokens, shard, output, keyval, sent, bound, held, sems):
-    count, both, width = sent.shape
+def cut_kernel(tokens, output, keyval, sent, bound, held, sems):
+    count, half, width = sent.shape
     head = output.shape[0]
-    sub = shard.shape[0] // count
-    half = both - sub
     start = pl.multiple_of(own_core() * half, half)
     copies = [
-        pltpu.make_async_copy(output, held.at[pl.ds(0, head), :], sems.at[2, 0]),
-        pltpu.make_async_copy(keyval, held.at[pl.ds(head, keyval.shape[0]), :], sems.at[2, 1]),
+        pltpu.make_async_copy(output, held.at[pl.ds(0, head), :], sems.at[1, 0]),
+        pltpu.make_async_copy(keyval, held.at[pl.ds(head, keyval.shape[0]), :], sems.at[1, 1]),
     ]
     for q in range(count):
         source = tokens.at[pl.ds(start, half), pl.ds(q * width, width)]
-        copies.append(pltpu.make_async_copy(source, sent.at[q, pl.ds(0, half)], sems.at[0, q]))
-        source = shard.at[pl.ds(q * sub, sub), :]
-        copies.append(pltpu.make_async_copy(source, sent.at[q, pl.ds(half, sub)], sems.at[1, q]))
+        copies.append(pltpu.make_async_copy(source, sent.at[q], sems.at[0, q]))
     for copy in copies:
         copy.start()
     for copy in copies[:2]:
         copy.wait()
-    save = pltpu.make_async_copy(held, bound, sems.at[2, 2])
+    save = pltpu.make_async_copy(held, bound, sems.at[1, 2])
     save.start()
     for copy in copies[2:]:
         copy.wait()
     save.wait()
 
 
-def cut(tokens, shard, output, keyval, count):
+def cut(tokens, output, keyval, count):
     rows, depth = tokens.shape
     together = (output.shape[0] + keyval.shape[0], output.shape[1])
-    outs = [bfloat(count, rows // 2 + shard.shape[0] // count, depth // count), bfloat(*together)]
-    scratch = [pltpu.VMEM(together, jnp.bfloat16), pltpu.SemaphoreType.DMA((3, max(3, count)))]
-    return call(cut_kernel, "cut", outs, [HBM] * 4, [tokens, shard, output, keyval], scratch, [VMEM, HBM])
+    outs = [bfloat(count, rows // 2, depth // count), bfloat(*together)]
+    scratch = [pltpu.VMEM(together, jnp.bfloat16), pltpu.SemaphoreType.DMA((2, max(3, count)))]
+    return call(cut_kernel, "cut", outs, [HBM] * 3, [tokens, output, keyval], scratch, [VMEM, HBM])
+
+
+def widen_kernel(query, keyval, wide, tall):
+    head, piece = query.shape[1], keyval.shape[0]
+    wide[:, :head] = query[...]
+    tall[:piece, :] = keyval[...]
+    tall[piece:, :] = jnp.zeros((LANES - piece, tall.shape[1]), tall.dtype)
+    for low in range(0, query.shape[0], LANES):
+        block = tall[:, low : low + LANES].astype(jnp.float32)
+        wide[low : low + LANES, head:] = jnp.transpose(block).astype(jnp.bfloat16)
+
+
+def widen(query, keyval):
+    depth, head = query.shape
+    scratch = [pltpu.VMEM((LANES, depth), jnp.bfloat16)]
+    outs = [bfloat(depth, head + LANES)]
+    return call(widen_kernel, "widen", outs, [VMEM] * 2, [query, keyval], scratch)[0]
 
 
 def norm_kernel(tokens, scale, whole, sems):
@@ -141,26 +150,36 @@
     return call(norm_kernel, "norms", outs, [HBM], [tokens], scratch)[0]
 
 
-def part_kernel(got, mine):
-    for q in range(mine.shape[0]):
-        mine[q] = got[q, : mine.shape[1], :]
-
-
-def part(got, half):
-    return call(part_kernel, "part", [bfloat(got.shape[0], half, got.shape[2])], [VMEM], [got])[0]
-
-
-def aim_kernel(got, heads, *pieces):
-    planes = len(pieces)
+def slice_kernel(shard, queries, *pieces):
+    count = len(pieces)
+    sub = pieces[0].shape[0]
+    for i in range(count):
+
+        @pl.when(lax.axis_index("inst") == i)
+        def give():
+            for d, piece in enumerate(pieces):
+                low = (i + d) % count * sub
+                piece[...] = shard[low : low + sub, :]
+
+
+def slices(shard, queries, count):
+    head, width = shard.shape
+    return call(slice_kernel, "slices", [bfloat(head // count, width)] * count, [VMEM] * 2, [shard, queries])
+
+
+def aim_kernel(count, *refs):
+    arrived, pieces, held = refs[:count], refs[count:-1], refs[-1]
+    for d, block in enumerate(arrived):
+        held[lax.rem(lax.axis_index("inst") - d + count, count)] = block[...]
     for e, piece in enumerate(pieces):
-        half = got.shape[1] - piece.shape[0]
-        piece[...] = got[lax.rem(lax.axis_index("tp") // 2 + e, planes), half:, :]
-
-
-def aim(got, half, heads):
-    planes = heads.shape[0]
-    outs = [bfloat(got.shape[1] - half, got.shape[2])] * planes
-    return call(aim_kernel, "aim", outs, [VMEM, VMEM], [got, heads])
+        piece[...] = held[lax.rem(lax.axis_index("tp") // 2 + e, len(pieces))]
+
+
+def aim(arrived, planes):
+    shape = arrived[0].shape
+    kernel = functools.partial(aim_kernel, len(arrived))
+    scratch = [pltpu.VMEM((len(arrived), *shape), jnp.bfloat16)]
+    return call(kernel, "aim", [bfloat(*shape)] * planes, [VMEM] * len(arrived), arrived, scratch)
 
 
 def keep_kernel(source, output, *refs):
@@ -176,42 +195,30 @@
     return call(keep_kernel, "keep", outs, ins, [block, output, *pieces], places=[VMEM, LAST])
 
 
-def fill_tall(keyval, tall):
-    piece = keyval.shape[0]
-    tall[:piece, :] = keyval[...]
-    tall[piece:, :] = jnp.zeros((LANES - piece, tall.shape[1]), tall.dtype)
-
-
-def project_kernel(mine, other, query, keyval, saved, sums, held, tall, sem):
-    count, half, _ = mine.shape
+def project_kernel(rows, weight, *refs):
+    first, (saved, sums, sem) = refs[:-3], refs[-3:]
+    count, half, width = rows.shape
+    save = pltpu.make_async_copy(rows, saved, sem)
+    save.start()
+    hidden = rows[...].reshape(count * half, width)
+    total = jnp.dot(hidden, weight[...], preferred_element_type=jnp.float32).astype(jnp.bfloat16)
     core = own_core()
     for q in range(count):
-        for source, place in ((mine, core), (other, 1 - core)):
-            held[pl.ds(pl.multiple_of((2 * q + place) * half, half), half), :] = source[q]
-    save = pltpu.make_async_copy(held, saved, sem)
-    save.start()
-    fill_tall(keyval, tall)
-    hidden = held[...]
-    head = query.shape[1]
-    queries = jnp.dot(hidden, query[...], preferred_element_type=jnp.float32).astype(jnp.bfloat16)
-    products = contract(hidden, tall[...], (1, 1)).astype(jnp.bfloat16)
-    for q in range(count):
-        sums[q, :, :head] = queries[2 * q * half : 2 * (q + 1) * half]
-        sums[q, :, head:] = products[2 * q * half : 2 * (q + 1) * half]
+        block = total[q * half : (q + 1) * half]
+        if first:
+            sums[q, pl.ds(pl.multiple_of(core * half, half), half), :] = first[0][q]
+            sums[q, pl.ds(pl.multiple_of((1 - core) * half, half), half), :] = block
+        else:
+            sums[q] = block
     save.wait()
 
 
-def project(mine, other, query, keyval):
-    count, half, width = mine.shape
-    rows = 2 * half
-    outs = [bfloat(count * rows, width), bfloat(count, rows, query.shape[1] + LANES)]
-    scratch = [
-        pltpu.VMEM((count * rows, width), jnp.bfloat16),
-        pltpu.VMEM((LANES, width), jnp.bfloat16),
-        pltpu.SemaphoreType.DMA(()),
-    ]
-    args = [mine, other, query, keyval]
-    return call(project_kernel, "project", outs, [VMEM] * 4, args, scratch, [HBM, VMEM])
+def project(rows, weight, *first):
+    count, half, width = rows.shape
+    outs = [bfloat(*rows.shape), bfloat(count, half * (1 + len(first)), weight.shape[1])]
+    args = [rows, weight, *first]
+    scratch = [pltpu.SemaphoreType.DMA(())]
+    return call(project_kernel, "project", outs, [VMEM] * len(args), args, scratch, [HBM, VMEM])
 
 
 def summed(parts):
@@ -252,7 +259,8 @@
     return contract(probabilities.astype(jnp.bfloat16), values_t, (1, dims[1])).astype(jnp.bfloat16)
 
 
-def first_kernel(queries, doc_ids, pieces, context):
+def first_kernel(queries, doc_ids, pieces, *refs):
+    context = refs[-1]
     span = pieces.shape[0] // 2
     keys_t = jnp.concatenate([pieces[g] for g in range(span)], 0)
     values_t = jnp.concatenate([pieces[g] for g in range(span, 2 * span)], 0)
@@ -261,9 +269,10 @@
         context[z] = result
 
 
-def first_attend(queries, doc_ids, pieces):
+def first_attend(queries, doc_ids, pieces, arrived):
     outs = [bfloat(lax.axis_size("tp") // 2, *queries.shape)]
-    return call(first_kernel, "attend", outs, [VMEM] * 3, [queries, doc_ids, pieces])[0]
+    args = [queries, doc_ids, pieces, *arrived]
+    return call(first_kernel, "attend", outs, [VMEM] * len(args), args)[0]
 
 
 def second_kernel(depth, head, rows, parts, doc_ids, sent):
@@ -315,17 +324,19 @@
                 left[at * rows : (at + 1) * rows, columns] = source[q, e]
 
 
-def advance_kernel(step, before, mine, other, output, query, sums, left, held, tall, hidden, blended, sems):
+def advance_kernel(step, own_rows, other_rows, mine, other, output, query, rows_by, sums, left, held, tall, hidden, blended, sems):
     count, pairs, rows, head = mine.shape
-    width = before.shape[1]
+    width = own_rows.shape[2]
     ranks = 2 * pairs
+    core = own_core()
     first = lax.axis_index("tp") // GROUP * GROUP
     copies = []
     for at in range(width // step):
         columns = pl.ds(at * step, step)
         pairs_of = [
             (output.at[:, pl.ds(0, head), columns], held.at[:, :, columns]),
-            (before.at[:, columns], hidden.at[:, columns]),
+            (own_rows.at[:, :, columns], hidden.at[:, core, :, columns]),
+            (other_rows.at[:, :, columns], hidden.at[:, 1 - core, :, columns]),
             (output.at[pl.ds(first, GROUP), pl.ds(head, tall.shape[1]), columns], tall.at[:, :, columns]),
         ]
         copies.append([pltpu.make_async_copy(*pair, sems.at[c, at]) for c, pair in enumerate(pairs_of)])
@@ -335,7 +346,7 @@
     for span in spans(count):
         place_contexts(mine, other, left, span)
         low, high = span[0] * rows, (span[-1] + 1) * rows
-        queries, keyvals, squares = 0.0, 0.0, 0.0
+        queries, keyvals, squares = 0.0, 0.0, jnp.zeros((high - low, LANES), jnp.float32)
         for at, chunk in enumerate(copies):
             if span[0] == 0:
                 for copy in chunk:
@@ -343,13 +354,17 @@
             columns = pl.ds(at * step, step)
             right = held[:, :, columns].reshape(ranks * head, step)
             attended = jnp.dot(left[: high - low, :], right, preferred_element_type=jnp.float32)
-            after_one = (hidden[low:high, columns].astype(jnp.float32) + attended).astype(jnp.bfloat16)
+            before = hidden[span[0] : span[-1] + 1, :, :, columns].reshape(high - low, step)
+            after_one = (before.astype(jnp.float32) + attended).astype(jnp.bfloat16)
             blended[low:high, columns] = after_one
             queries = queries + jnp.dot(after_one, query[columns, :], preferred_element_type=jnp.float32)
             right = tall[:, :, columns].reshape(GROUP * tall.shape[1], step)
             keyvals = keyvals + contract(after_one, right, (1, 1))
             floats = after_one.astype(jnp.float32)
-            squares = squares + jnp.sum(floats * floats, axis=1, keepdims=True)
+            for lane in range(0, step, LANES):
+                part = floats[:, lane : lane + LANES]
+                squares = squares + part * part
+        squares = jnp.sum(squares, axis=1, keepdims=True)
         queries, keyvals = queries.astype(jnp.bfloat16), keyvals.astype(jnp.bfloat16)
         for at, q in enumerate(span):
             slot = (q + 1) % count
@@ -378,66 +393,64 @@
                     sums[(q + 1) % count, :rows, wide + b * slim : wide + (b + 1) * slim] = block
 
 
-def advance(before, mine, other, output, query):
+def advance(own_rows, other_rows, mine, other, output, query, rows_by):
     count, pairs, rows, head = mine.shape
-    total, width = before.shape
+    width = own_rows.shape[2]
+    total = count * rows
     step = min(512, width)
     ranks, both, _ = output.shape
     scratch = [
         pltpu.VMEM((min(4, count) * rows, ranks * head), jnp.bfloat16),
         pltpu.VMEM((ranks, head, width), jnp.bfloat16),
         pltpu.VMEM((GROUP, both - head, width), jnp.bfloat16),
+        pltpu.VMEM((count, 2, rows // 2, width), jnp.bfloat16),
         pltpu.VMEM((total, width), jnp.bfloat16),
-        pltpu.VMEM((total, width), jnp.bfloat16),
-        pltpu.SemaphoreType.DMA((3, width // step)),
+        pltpu.SemaphoreType.DMA((4, width // step)),
     ]
     outs = [bfloat(count, rows + 16, 3 * head + width // ranks)]
-    ins = [HBM] + [VMEM] * 2 + [HBM, VMEM]
-    args = [before, mine, other, output, query]
+    ins = [HBM] * 2 + [VMEM] * 2 + [HBM, VMEM, HBM]
+    args = [own_rows, other_rows, mine, other, output, query, rows_by]
     return call(functools.partial(advance_kernel, step), "advance", outs, ins, args, scratch)[0]
 
 
-def blend_kernel(got, rows_by, kept, sent, held, sems):
+def blend_kernel(swap, got, rows_by, out, held, sems):
     pairs, rows, _ = got.shape
     count, _, sub, _ = rows_by.shape
     head = count * sub
     plane = lax.axis_index("tp") // 2
+    half = out.shape[1]
+    slim = half // (2 * pairs)
+    core = own_core()
+    place = 1 - core if swap else core
     copies = []
     for i in range(count):
         for e in range(pairs):
+            source = rows_by.at[i, e, :, pl.ds(pl.multiple_of(place * half, half), half)]
             target = held.at[pl.ds(e * head + i * sub, sub), :]
-            copies.append(pltpu.make_async_copy(rows_by.at[i, e], target, sems.at[i, e]))
+            copies.append(pltpu.make_async_copy(source, target, sems.at[i, e]))
     for copy in copies:
         copy.start()
     left = jnp.concatenate([got[lax.rem(plane - e + pairs, pairs), :, :head] for e in range(pairs)], 1)
-    half = kept.shape[1]
-    slim = half // (2 * pairs)
+    rest = []
+    for a in range(pairs):
+        low = got[a, :, head : head + slim]
+        high = got[a, :, head + slim : head + 2 * slim]
+        ours = jnp.where(place == 0, low, high).astype(jnp.float32)
+        rest += [jnp.where(core == 0, ours, 0.0), jnp.where(core == 0, 0.0, ours)]
+    rest = jnp.concatenate(rest, 1)
     for copy in copies:
         copy.wait()
-    for core in range(2):
-
-        @pl.when(own_core() == core)
-        def give():
-            for b in range(2):
-                rest = []
-                for a in range(pairs):
-                    ours = got[a, :, head + b * slim : head + (b + 1) * slim]
-                    rest += [ours, jnp.zeros_like(ours)] if core == 0 else [jnp.zeros_like(ours), ours]
-                rest = jnp.concatenate(rest, 1).astype(jnp.float32)
-                right = held[:, b * half : (b + 1) * half]
-                total = jnp.dot(left, right, preferred_element_type=jnp.float32) + rest
-                if b == core:
-                    kept[...] = total
-                else:
-                    sent[...] = total.astype(jnp.bfloat16)
-
-
-def blend(got, rows_by):
+    total = jnp.dot(left, held[...], preferred_element_type=jnp.float32) + rest
+    out[...] = total.astype(out.dtype)
+
+
+def blend(got, rows_by, swap):
     pairs, rows, _ = got.shape
     count, _, sub, width = rows_by.shape
-    scratch = [pltpu.VMEM((pairs * count * sub, width), jnp.bfloat16), pltpu.SemaphoreType.DMA((count, pairs))]
-    outs = [jax.ShapeDtypeStruct((rows, width // 2), jnp.float32), bfloat(rows, width // 2)]
-    return call(blend_kernel, "blend", outs, [VMEM, HBM], [got, rows_by], scratch)
+    scratch = [pltpu.VMEM((pairs * count * sub, width // 2), jnp.bfloat16), pltpu.SemaphoreType.DMA((count, pairs))]
+    outs = [jax.ShapeDtypeStruct((rows, width // 2), jnp.bfloat16 if swap else jnp.float32)]
+    kernel = functools.partial(blend_kernel, swap)
+    return call(kernel, "blend", outs, [VMEM, HBM], [got, rows_by], scratch)[0]
 
 
 def join_kernel(kept, arrived, blended):
@@ -456,23 +469,27 @@
     if ranks > GROUP:
         groups = [list(range(low, low + GROUP)) for low in range(0, ranks, GROUP)]
 
-    sent, bound = cut(tokens, output_two, output_one, keyval_two.T, count)
+    sent, bound = cut(tokens, output_one, keyval_two.T, count)
     output_all = lax.all_gather(bound, "tp", axis=0)
-    got = exchange(sent, "inst")
-    mine = part(got, rows // 2)
-    held, sums = project(mine, other_core(mine), query_one, keyval_one.T)
+    mine = exchange(sent, "inst")
+    weight = widen(query_one, keyval_one.T)
+    own_rows, first = project(mine, weight)
+    other_rows, sums = project(other_core(mine), weight, first)
     queries, keyvals_t = finish(exchange(sums, "inst"), norms(tokens), head, piece)
-    context = first_attend(queries, doc_ids, exchange(keyvals_t, "tp", groups))
+    arrived = slices(output_two, queries, count)
+    arrived = [arrived[0]] + [shifted(arrived[d], "inst", d) for d in range(1, count)]
+    pieces = aim(arrived, ranks // 2)
+    pieces = [pieces[0]] + [shifted(pieces[e], "tp", 2 * e) for e in range(1, ranks // 2)]
+    context = first_attend(queries, doc_ids, exchange(keyvals_t, "tp", groups), arrived)
     heads = exchange(context, "tp", core_groups())
-    pieces = aim(got, rows // 2, heads)
-    pieces = [pieces[0]] + [shifted(pieces[e], "tp", 2 * e) for e in range(1, ranks // 2)]
     mine, rows_by = keep(exchange(spread(heads), "inst"), output_all, pieces)
+    sums = advance(own_rows, other_rows, mine, other_core(mine), output_all, query_two, rows_by)
     rows_by = lax.all_gather(rows_by, "inst", axis=0)
-    sums = advance(held, mine, other_core(mine), output_all, query_two)
 
     sent = second_attend(exchange(sums, "inst"), doc_ids, depth, head)
-    kept, sent = blend(exchange(sent, "tp", core_groups()), rows_by)
-    return join(kept, other_core(sent))
+    got = exchange(sent, "tp", core_groups())
+    arrived = other_core(blend(got, rows_by, True))
+    return join(blend(got, rows_by, False), arrived)
 
 
 def solution(mesh):

time: 154 us -> 148 us (0.961)
  blocking collectives: 84.1 us -> 64.4 us
  starting transfers between devices: 16.4 us -> 25.7 us
  waiting for transfers between devices: 17.7 us -> 20.8 us
  Pallas kernels: 20.6 us -> 22.5 us
    all_to_all x5 -> x4, blocking collectives: 84.1 us -> 64.4 us  [exchange(): return lax.all_to_all(block, axis, 0, 0, axis_index_groups=groups)]
    all_to_all x2 -> x3, starting transfers between devices: 6.95 us -> 12.9 us  [exchange(): return lax.all_to_all(block, axis, 0, 0, axis_index_groups=groups)]
    ppermute x3 -> x6, waiting for transfers between devices: 8.28 us -> 14.1 us  [shifted(): lax.ppermute(block, axis, [(s, (s + distance) % count) for s in range(cou...]
    ppermute x3 -> x6, starting transfers between devices: 3.8 us -> 7.41 us  [shifted(): lax.ppermute(block, axis, [(s, (s + distance) % count) for s in range(cou...]
    ppermute x3, waiting for transfers between devices: 5.64 us -> 2.68 us  [other_core(): return lax.ppermute(block, 'tp', [(s, s ^ 1) for s in range(count)])]
    pallas_call x13 -> x16, Pallas kernels: 20.6 us -> 22.5 us  [call(): pl.pallas_call(kernel, out_shape=outs, in_specs=ins, out_specs=[VMEM if s...]
    all_to_all x2 -> x3, waiting for transfers between devices: 3.77 us -> 3.99 us  [exchange(): return lax.all_to_all(block, axis, 0, 0, axis_index_groups=groups)]
  transfers between devices with their start and end apart: 10 -> 14, of which waited for: 6 -> 8; matrix products, arithmetic and copies ran while one was open for 0% -> 0% of each run, Pallas kernels for 9% -> 12%
where the time goes in v2:
time: 148 us; the launch traced here: 147 us
  blocking collectives  64.4 us (44%)
  starting transfers between devices  25.7 us (17%)
  Pallas kernels  22.5 us (15%)
  waiting for transfers between devices  20.8 us (14%)
  between operations  13.6 us (9%)
    all_to_all x4, blocking collectives, exchange(): return lax.all_to_all(block, axis, 0, 0, axis_index_groups=groups)  64.4 us
    pallas_call x16, Pallas kernels, call(): pl.pallas_call(kernel, out_shape=outs, in_specs=ins, out_specs=[VMEM if s...  22.5 us
    ppermute x6, waiting for transfers between devices, shifted(): lax.ppermute(block, axis, [(s, (s + distance) % count) for s in range(cou...  14.1 us
    all_to_all x3, starting transfers between devices, exchange(): return lax.all_to_all(block, axis, 0, 0, axis_index_groups=groups)  12.9 us
    ppermute x6, starting transfers between devices, shifted(): lax.ppermute(block, axis, [(s, (s + distance) % count) for s in range(cou...  7.41 us
    ppermute x3, starting transfers between devices, other_core(): return lax.ppermute(block, 'tp', [(s, s ^ 1) for s in range(count)])  5.31 us
    all_to_all x3, waiting for transfers between devices, exchange(): return lax.all_to_all(block, axis, 0, 0, axis_index_groups=groups)  3.99 us
  transfers between devices with their start and end apart: 14, of which 8 were waited for; matrix products, arithmetic and copies ran while one was open for 0% of the time, Pallas kernels for 12%

profile of v2, /device:TPU:1, one launch (start us, length us, event | category | flops | bytes accessed | tf_op | source)
XLA Modules:
  0.0 147.0 jit_solution(8978281749526293479)
XLA Ops:
  6.5 0.0 all-gather.5.cloned.1.call-start
  6.5 2.0 %cut.1 = (bf16[4,80,2048]{2,1,0:T(8,128)(2,1)S(1)}, bf16[160,2048]{1,0:T(8,128)(2,1)}) custom-call(bf16[160,8192]{1,0:T(8,128)(2,1)} %tokens.3, bf16[128,2048]{1,0:T(8,128)(2,1)} %output.1, bf16[32,2048]{1,0:T(8,128)(2,1)} %bitcast.9), custom_call_target="tpu_custom_call" | custom-call | tf_op jit(solution)/shard_map/cut/pallas_call | solution.py:56
  8.5 0.0 all-gather.5.cloned.1.call-update
  8.6 0.0 copy-start.1
  8.6 0.0 copy-start.3
  8.6 20.0 %all_to_all.35.rows = bf16[4,80,2048]{2,1,0:T(8,128)(2,1)S(1)} all-to-all(bf16[4,80,2048]{2,1,0:T(8,128)(2,1)S(1)} %get-tuple-element.23), channel_id=1, replica_groups=mesh['inst'=4,'tp'=8] {'inst'}, dimensions={0} | all-to-all | bytes 2621440 | tf_op jit(solution)/shard_map/all_to_all | solution.py:24
  28.6 2.1 %collective-permute-start = (bf16[4,80,2048]{2,1,0:T(8,128)(2,1)S(1)}, bf16[4,80,2048]{2,1,0:T(8,128)(2,1)S(1)}, u32[]{:S(2)}, u32[]{:S(2)}) collective-permute-start(bf16[4,80,2048]{2,1,0:T(8,128)(2,1)S(1)} %all_to_all.35.rows), channel_id=1, source_target_pairs={{0,1},{1,0},{2,3},{3,2},{4,5},{5,4},{6,7},{7,6},{8,9},{9,8},{10,11... | collective-permute-start | bytes 3932168 | tf_op jit(solution)/shard_map/ppermute | solution.py:29
  30.7 0.0 copy-done.1
  30.7 0.0 copy-done.3
  30.7 0.3 widen.1.weight
  31.0 1.4 project.2
  32.4 1.0 collective-permute-done.rows
  33.3 1.9 %project.3 = (bf16[4,80,2048]{2,1,0:T(8,128)(2,1)}, bf16[4,160,256]{2,1,0:T(8,128)(2,1)}) custom-call(bf16[4,80,2048]{2,1,0:T(8,128)(2,1)S(1)} %collective-permute-done.rows, bf16[2048,256]{1,0:T(8,128)(2,1)S(1)} %widen.1.weight, bf16[4,80,256]{2,1,0:T(8,128)(2,1)S(1)} %get-tuple-element.25.refs_0_), custom_call_target="tpu_custom_call" | custom-call | tf_op jit(solution)/shard_map/project/pallas_call | solution.py:56
  35.3 3.5 %all-to-all-start.1 = ((bf16[4,160,256]{2,1,0:T(8,128)(2,1)}), bf16[4,160,256]{2,1,0:T(8,128)(2,1)S(1)}, u32[]{:S(2)}, u32[]{:S(2)}) async-start(bf16[4,160,256]{2,1,0:T(8,128)(2,1)} %get-tuple-element.27), calls=%async_computation.1 | async-start | bytes 655360 | tf_op jit(solution)/shard_map/all_to_all | solution.py:24
  38.7 0.0 copy-start.2
  38.8 0.0 copy-start.4
  38.8 2.0 %norms.1.scale = f32[160,1]{1,0:T(8,128)S(1)} custom-call(bf16[160,8192]{1,0:T(8,128)(2,1)} %tokens.3), custom_call_target="tpu_custom_call" | custom-call | tf_op jit(solution)/shard_map/norms/pallas_call | solution.py:56
  40.8 3.7 %all-to-all-done.1.parts = bf16[4,160,256]{2,1,0:T(8,128)(2,1)S(1)} async-done(((bf16[4,160,256]{2,1,0:T(8,128)(2,1)}), bf16[4,160,256]{2,1,0:T(8,128)(2,1)S(1)}, u32[]{:S(2)}, u32[]{:S(2)}) %all-to-all-start.1) | async-done | bytes 327712 | tf_op jit(solution)/shard_map/all_to_all | solution.py:24
  44.5 0.9 finish.1
  45.4 6.0 %all-to-all-start.2 = ((bf16[8,32,160]{2,1,0:T(8,128)(2,1)}), bf16[8,32,160]{2,1,0:T(8,128)(2,1)S(1)}, u32[]{:S(2)}, u32[]{:S(2)}) async-start(bf16[8,32,160]{2,1,0:T(8,128)(2,1)} %get-tuple-element.29), calls=%async_computation.2 | async-start | bytes 262144 | tf_op jit(solution)/shard_map/all_to_all | solution.py:24
  51.3 0.0 copy-done.2
  51.4 1.2 collective-permute-start.1
  52.6 0.3 collective-permute-start.2
  52.9 2.1 %collective-permute-start.3 = (bf16[32,2048]{1,0:T(8,128)(2,1)S(1)}, bf16[32,2048]{1,0:T(8,128)(2,1)S(1)}, u32[]{:S(2)}, u32[]{:S(2)}) collective-permute-start(bf16[32,2048]{1,0:T(8,128)(2,1)S(1)} %get-tuple-element.33), channel_id=1, source_target_pairs={{0,24},{8,0},{16,8},{24,16},{1,25},{9,1},{17,9},{25,17},{2,26},{10... | collective-permute-start | bytes 393224 | tf_op jit(solution)/shard_map/ppermute | solution.py:73
  55.0 2.6 %collective-permute-done.1.refs_1_ = bf16[32,2048]{1,0:T(8,128)(2,1)S(1)} collective-permute-done((bf16[32,2048]{1,0:T(8,128)(2,1)S(1)}, bf16[32,2048]{1,0:T(8,128)(2,1)S(1)}, u32[]{:S(2)}, u32[]{:S(2)}) %collective-permute-start.1) | collective-permute-done | bytes 131104 | tf_op jit(solution)/shard_map/ppermute | solution.py:73
  57.6 3.1 %collective-permute-done.2.refs_2_ = bf16[32,2048]{1,0:T(8,128)(2,1)S(1)} collective-permute-done((bf16[32,2048]{1,0:T(8,128)(2,1)S(1)}, bf16[32,2048]{1,0:T(8,128)(2,1)S(1)}, u32[]{:S(2)}, u32[]{:S(2)}) %collective-permute-start.2) | collective-permute-done | bytes 131104 | tf_op jit(solution)/shard_map/ppermute | solution.py:73
  60.7 0.0 collective-permute-done.3.refs_3_
  60.7 0.3 all-to-all-done.2.pieces
  61.0 0.0 copy-done.4
  61.0 0.5 attend.2
  61.5 9.5 %all_to_all.36.heads = bf16[4,160,128]{2,1,0:T(8,128)(2,1)S(1)} all-to-all(bf16[4,160,128]{2,1,0:T(8,128)(2,1)S(1)} %attend.2), channel_id=1, replica_groups={{0,2,4,6},{1,3,5,7},{8,10,12,14},{9,11,13,15},{16,18,20,22},{17,19,21,2..., dimensions={0} | all-to-all | bytes 327680 | tf_op jit(solution)/shard_map/all_to_all | solution.py:24
  71.0 0.9 spread.1
  71.9 3.5 %all-to-all-start.4 = ((bf16[4,4,160,128]{3,2,1,0:T(8,128)(2,1)}), bf16[4,4,160,128]{3,2,1,0:T(8,128)(2,1)S(1)}, u32[]{:S(2)}, u32[]{:S(2)}) async-start(bf16[4,4,160,128]{3,2,1,0:T(8,128)(2,1)} %spread.1), calls=%async_computation.4 | async-start | bytes 1310720 | tf_op jit(solution)/shard_map/all_to_all | solution.py:24
  75.4 0.0 all-gather.7.cloned.1.call-start
  75.4 0.1 aim.1
  75.5 0.6 collective-permute-start.4
  76.2 2.2 %collective-permute-start.5 = (bf16[32,2048]{1,0:T(8,128)(2,1)S(1)}, bf16[32,2048]{1,0:T(8,128)(2,1)S(1)}, u32[]{:S(2)}, u32[]{:S(2)}) collective-permute-start(bf16[32,2048]{1,0:T(8,128)(2,1)S(1)} %get-tuple-element.37), channel_id=1, source_target_pairs={{0,4},{1,5},{2,6},{3,7},{4,0},{5,1},{6,2},{7,3},{8,12},{9,13},{10,... | collective-permute-start | bytes 393224 | tf_op jit(solution)/shard_map/ppermute | solution.py:73
  78.3 1.0 collective-permute-start.6
  79.3 2.0 %collective-permute-done.4.refs_1_ = bf16[32,2048]{1,0:T(8,128)(2,1)S(1)} collective-permute-done((bf16[32,2048]{1,0:T(8,128)(2,1)S(1)}, bf16[32,2048]{1,0:T(8,128)(2,1)S(1)}, u32[]{:S(2)}, u32[]{:S(2)}) %collective-permute-start.4) | collective-permute-done | bytes 131104 | tf_op jit(solution)/shard_map/ppermute | solution.py:73
  81.4 6.4 %collective-permute-done.5.refs_2_ = bf16[32,2048]{1,0:T(8,128)(2,1)S(1)} collective-permute-done((bf16[32,2048]{1,0:T(8,128)(2,1)S(1)}, bf16[32,2048]{1,0:T(8,128)(2,1)S(1)}, u32[]{:S(2)}, u32[]{:S(2)}) %collective-permute-start.5) | collective-permute-done | bytes 131104 | tf_op jit(solution)/shard_map/ppermute | solution.py:73
  87.8 0.0 collective-permute-done.6.refs_3_
  87.8 0.0 all-to-all-done.4.source
  87.8 0.0 all-gather.5.cloned.1.call-done
  87.8 0.0 copy-start
  87.8 0.9 keep.1
  88.7 0.0 all-gather.7.cloned.1.call-update
  88.7 1.4 collective-permute-start.7
  90.2 1.7 %collective-permute-done.7.other = bf16[4,4,160,128]{3,2,1,0:T(8,128)(2,1)S(1)} collective-permute-done((bf16[4,4,160,128]{3,2,1,0:T(8,128)(2,1)S(1)}, bf16[4,4,160,128]{3,2,1,0:T(8,128)(2,1)S(1)}, u32[]{:S(2)}, u32[]{:S(2)}) %collective-permute-start.7) | collective-permute-done | bytes 655392 | tf_op jit(solution)/shard_map/ppermute | solution.py:29
  91.9 0.0 copy-done
  91.9 6.8 %advance.1 = bf16[4,176,640]{2,1,0:T(8,128)(2,1)S(1)} custom-call(bf16[4,80,2048]{2,1,0:T(8,128)(2,1)} %get-tuple-element.24.own_rows, bf16[4,80,2048]{2,1,0:T(8,128)(2,1)} %get-tuple-element.26.other_rows, bf16[4,4,160,128]{3,2,1,0:T(8,128)(2,1)S(1)} %get-tuple-element.39.mine, bf16[4,4,160,128]{3,2,1,0:T(8,128)(2,1)S(1)} %collective-permute-done.7.other, ...), custom_call_target="tpu_custom_call" | custom-call | tf_op jit(solution)/shard_map/advance/pallas_call | solution.py:56
  98.7 17.8 %all_to_all.37.parts = bf16[4,176,640]{2,1,0:T(8,128)(2,1)S(1)} all-to-all(bf16[4,176,640]{2,1,0:T(8,128)(2,1)S(1)} %advance.1), channel_id=1, replica_groups=mesh['inst'=4,'tp'=8] {'inst'}, dimensions={0} | all-to-all | bytes 1802240 | tf_op jit(solution)/shard_map/all_to_all | solution.py:24
  116.5 0.6 attend.3
  117.0 17.1 %all_to_all.38.got = bf16[4,160,384]{2,1,0:T(8,128)(2,1)S(1)} all-to-all(bf16[4,160,384]{2,1,0:T(8,128)(2,1)S(1)} %attend.3), channel_id=1, replica_groups={{0,2,4,6},{1,3,5,7},{8,10,12,14},{9,11,13,15},{16,18,20,22},{17,19,21,2..., dimensions={0} | all-to-all | bytes 983040 | tf_op jit(solution)/shard_map/all_to_all | solution.py:24
  134.1 0.0 all-gather.7.cloned.1.call-done
  134.2 1.7 %blend.3 = bf16[160,1024]{1,0:T(8,128)(2,1)S(1)} custom-call(bf16[4,160,384]{2,1,0:T(8,128)(2,1)S(1)} %all_to_all.38.got, bf16[4,4,32,2048]{3,2,1,0:T(8,128)(2,1)} %bitcast.7), custom_call_target="tpu_custom_call" | custom-call | tf_op jit(solution)/shard_map/blend/pallas_call | solution.py:56
  135.9 1.8 %collective-permute-start.8 = (bf16[160,1024]{1,0:T(8,128)(2,1)S(1)}, bf16[160,1024]{1,0:T(8,128)(2,1)S(1)}, u32[]{:S(2)}, u32[]{:S(2)}) collective-permute-start(bf16[160,1024]{1,0:T(8,128)(2,1)S(1)} %blend.3), channel_id=1, source_target_pairs={{0,1},{1,0},{2,3},{3,2},{4,5},{5,4},{6,7},{7,6},{8,9},{9,8},{10,11... | collective-permute-start | bytes 983048 | tf_op jit(solution)/shard_map/ppermute | solution.py:29
  137.7 1.7 %blend.2.kept = f32[160,1024]{1,0:T(8,128)S(1)} custom-call(bf16[4,160,384]{2,1,0:T(8,128)(2,1)S(1)} %all_to_all.38.got, bf16[4,4,32,2048]{3,2,1,0:T(8,128)(2,1)} %bitcast.8), custom_call_target="tpu_custom_call" | custom-call | tf_op jit(solution)/shard_map/blend/pallas_call | solution.py:56
  139.4 0.0 collective-permute-done.8.arrived
  139.4 0.8 join.1
  (1 shorter events, 0.0 us)
Async XLA Ops:
  6.5 81.2 %all-gather.5.cloned.1.call-start = ((), (), s32[]{:S(2)}) async-start(), calls=%async_computation.7 | async-start | bytes 5898240 | tf_op jit(solution)/shard_map/all_gather | solution.py:473
  8.6 22.1 %copy-start.1 = (bf16[2048,128]{1,0:T(8,128)(2,1)S(1)}, bf16[2048,128]{1,0:T(8,128)(2,1)}, u32[]{:S(2)}) copy-start(bf16[2048,128]{1,0:T(8,128)(2,1)} %query.2) | copy-start | bytes 1572868
  8.6 22.1 %copy-start.3 = (bf16[2048,32]{0,1:T(8,128)(2,1)S(1)}, bf16[2048,32]{0,1:T(8,128)(2,1)}, u32[]{:S(2)}) copy-start(bf16[2048,32]{0,1:T(8,128)(2,1)} %param.11) | copy-start | bytes 393220
  28.6 4.8 %collective-permute-start = (bf16[4,80,2048]{2,1,0:T(8,128)(2,1)S(1)}, bf16[4,80,2048]{2,1,0:T(8,128)(2,1)S(1)}, u32[]{:S(2)}, u32[]{:S(2)}) collective-permute-start(bf16[4,80,2048]{2,1,0:T(8,128)(2,1)S(1)} %all_to_all.35.rows), channel_id=1, source_target_pairs={{0,1},{1,0},{2,3},{3,2},{4,5},{5,4},{6,7},{7,6},{8,9},{9,8},{10,11... | collective-permute-start | bytes 3932168 | tf_op jit(solution)/shard_map/ppermute | solution.py:29
  35.3 9.2 %all-to-all-start.1 = ((bf16[4,160,256]{2,1,0:T(8,128)(2,1)}), bf16[4,160,256]{2,1,0:T(8,128)(2,1)S(1)}, u32[]{:S(2)}, u32[]{:S(2)}) async-start(bf16[4,160,256]{2,1,0:T(8,128)(2,1)} %get-tuple-element.27), calls=%async_computation.1 | async-start | bytes 655360 | tf_op jit(solution)/shard_map/all_to_all | solution.py:24
  38.7 12.6 %copy-start.2 = (bf16[128,2048]{1,0:T(8,128)(2,1)S(1)}, bf16[128,2048]{1,0:T(8,128)(2,1)}, u32[]{:S(2)}) copy-start(bf16[128,2048]{1,0:T(8,128)(2,1)} %shard.1) | copy-start | bytes 1572868
  38.8 22.2 %copy-start.4 = (s32[4,160]{1,0:T(4,128)S(1)}, s32[4,160]{1,0:T(4,128)}, u32[]{:S(2)}) copy-start(s32[4,160]{1,0:T(4,128)} %doc_ids.3) | copy-start | bytes 7684
  45.4 15.6 %all-to-all-start.2 = ((bf16[8,32,160]{2,1,0:T(8,128)(2,1)}), bf16[8,32,160]{2,1,0:T(8,128)(2,1)S(1)}, u32[]{:S(2)}, u32[]{:S(2)}) async-start(bf16[8,32,160]{2,1,0:T(8,128)(2,1)} %get-tuple-element.29), calls=%async_computation.2 | async-start | bytes 262144 | tf_op jit(solution)/shard_map/all_to_all | solution.py:24
  51.4 6.2 %collective-permute-start.1 = (bf16[32,2048]{1,0:T(8,128)(2,1)S(1)}, bf16[32,2048]{1,0:T(8,128)(2,1)S(1)}, u32[]{:S(2)}, u32[]{:S(2)}) collective-permute-start(bf16[32,2048]{1,0:T(8,128)(2,1)S(1)} %get-tuple-element.31), channel_id=1, source_target_pairs={{0,8},{8,16},{16,24},{24,0},{1,9},{9,17},{17,25},{25,1},{2,10},{10... | collective-permute-start | bytes 393224 | tf_op jit(solution)/shard_map/ppermute | solution.py:73
  52.6 8.1 %collective-permute-start.2 = (bf16[32,2048]{1,0:T(8,128)(2,1)S(1)}, bf16[32,2048]{1,0:T(8,128)(2,1)S(1)}, u32[]{:S(2)}, u32[]{:S(2)}) collective-permute-start(bf16[32,2048]{1,0:T(8,128)(2,1)S(1)} %get-tuple-element.32), channel_id=1, source_target_pairs={{0,16},{8,24},{16,0},{24,8},{1,17},{9,25},{17,1},{25,9},{2,18},{10... | collective-permute-start | bytes 393224 | tf_op jit(solution)/shard_map/ppermute | solution.py:73
  52.9 7.8 %collective-permute-start.3 = (bf16[32,2048]{1,0:T(8,128)(2,1)S(1)}, bf16[32,2048]{1,0:T(8,128)(2,1)S(1)}, u32[]{:S(2)}, u32[]{:S(2)}) collective-permute-start(bf16[32,2048]{1,0:T(8,128)(2,1)S(1)} %get-tuple-element.33), channel_id=1, source_target_pairs={{0,24},{8,0},{16,8},{24,16},{1,25},{9,1},{17,9},{25,17},{2,26},{10... | collective-permute-start | bytes 393224 | tf_op jit(solution)/shard_map/ppermute | solution.py:73
  71.9 15.9 %all-to-all-start.4 = ((bf16[4,4,160,128]{3,2,1,0:T(8,128)(2,1)}), bf16[4,4,160,128]{3,2,1,0:T(8,128)(2,1)S(1)}, u32[]{:S(2)}, u32[]{:S(2)}) async-start(bf16[4,4,160,128]{3,2,1,0:T(8,128)(2,1)} %spread.1), calls=%async_computation.4 | async-start | bytes 1310720 | tf_op jit(solution)/shard_map/all_to_all | solution.py:24
  75.4 58.8 %all-gather.7.cloned.1.call-start = ((), (), s32[]{:S(2)}) async-start(), calls=%async_computation.8 | async-start | bytes 2621440 | tf_op jit(solution)/shard_map/all_gather | solution.py:487
  75.5 5.8 %collective-permute-start.4 = (bf16[32,2048]{1,0:T(8,128)(2,1)S(1)}, bf16[32,2048]{1,0:T(8,128)(2,1)S(1)}, u32[]{:S(2)}, u32[]{:S(2)}) collective-permute-start(bf16[32,2048]{1,0:T(8,128)(2,1)S(1)} %get-tuple-element.36), channel_id=1, source_target_pairs={{0,2},{1,3},{2,4},{3,5},{4,6},{5,7},{6,0},{7,1},{8,10},{9,11},{10,... | collective-permute-start | bytes 393224 | tf_op jit(solution)/shard_map/ppermute | solution.py:73
  76.2 11.6 %collective-permute-start.5 = (bf16[32,2048]{1,0:T(8,128)(2,1)S(1)}, bf16[32,2048]{1,0:T(8,128)(2,1)S(1)}, u32[]{:S(2)}, u32[]{:S(2)}) collective-permute-start(bf16[32,2048]{1,0:T(8,128)(2,1)S(1)} %get-tuple-element.37), channel_id=1, source_target_pairs={{0,4},{1,5},{2,6},{3,7},{4,0},{5,1},{6,2},{7,3},{8,12},{9,13},{10,... | collective-permute-start | bytes 393224 | tf_op jit(solution)/shard_map/ppermute | solution.py:73
  78.3 9.4 %collective-permute-start.6 = (bf16[32,2048]{1,0:T(8,128)(2,1)S(1)}, bf16[32,2048]{1,0:T(8,128)(2,1)S(1)}, u32[]{:S(2)}, u32[]{:S(2)}) collective-permute-start(bf16[32,2048]{1,0:T(8,128)(2,1)S(1)} %get-tuple-element.38), channel_id=1, source_target_pairs={{0,6},{1,7},{2,0},{3,1},{4,2},{5,3},{6,4},{7,5},{8,14},{9,15},{10,... | collective-permute-start | bytes 393224 | tf_op jit(solution)/shard_map/ppermute | solution.py:73
  87.8 4.1 %copy-start = (bf16[2048,128]{1,0:T(8,128)(2,1)S(1)}, bf16[2048,128]{1,0:T(8,128)(2,1)}, u32[]{:S(2)}) copy-start(bf16[2048,128]{1,0:T(8,128)(2,1)} %query.3) | copy-start | bytes 1572868
  88.7 3.1 %collective-permute-start.7 = (bf16[4,4,160,128]{3,2,1,0:T(8,128)(2,1)S(1)}, bf16[4,4,160,128]{3,2,1,0:T(8,128)(2,1)S(1)}, u32[]{:S(2)}, u32[]{:S(2)}) collective-permute-start(bf16[4,4,160,128]{3,2,1,0:T(8,128)(2,1)S(1)} %get-tuple-element.39.mine), channel_id=1, source_target_pairs={{0,1},{1,0},{2,3},{3,2},{4,5},{5,4},{6,7},{7,6},{8,9},{9,8},{10,11... | collective-permute-start | bytes 1966088 | tf_op jit(solution)/shard_map/ppermute | solution.py:29
  135.9 3.5 %collective-permute-start.8 = (bf16[160,1024]{1,0:T(8,128)(2,1)S(1)}, bf16[160,1024]{1,0:T(8,128)(2,1)S(1)}, u32[]{:S(2)}, u32[]{:S(2)}) collective-permute-start(bf16[160,1024]{1,0:T(8,128)(2,1)S(1)} %blend.3), channel_id=1, source_target_pairs={{0,1},{1,0},{2,3},{3,2},{4,5},{5,4},{6,7},{7,6},{8,9},{9,8},{10,11... | collective-permute-start | bytes 983048 | tf_op jit(solution)/shard_map/ppermute | solution.py:29
Sparse Core Ops, SparseCore 0:
  9.0 61.3 all-gather.4
  88.9 42.3 all-gather.6

commit v3 on v2

--- a/solution.py
+++ b/solution.py
@@ -397,7 +397,7 @@
     count, pairs, rows, head = mine.shape
     width = own_rows.shape[2]
     total = count * rows
-    step = min(512, width)
+    step = min(1024, width)
     ranks, both, _ = output.shape
     scratch = [
         pltpu.VMEM((min(4, count) * rows, ranks * head), jnp.bfloat16),

time: 148 us -> 148 us (level)
  no operation moved by 1% of the time
where the time goes in v3:
time: 148 us; the launch traced here: 147 us
  blocking collectives  64.2 us (43%)
  starting transfers between devices  25.7 us (17%)
  Pallas kernels  22.7 us (15%)
  waiting for transfers between devices  20.8 us (14%)
  between operations  13.6 us (9%)
    all_to_all x4, blocking collectives, exchange(): return lax.all_to_all(block, axis, 0, 0, axis_index_groups=groups)  64.2 us
    pallas_call x16, Pallas kernels, call(): pl.pallas_call(kernel, out_shape=outs, in_specs=ins, out_specs=[VMEM if s...  22.7 us
    ppermute x6, waiting for transfers between devices, shifted(): lax.ppermute(block, axis, [(s, (s + distance) % count) for s in range(cou...  14.1 us
    all_to_all x3, starting transfers between devices, exchange(): return lax.all_to_all(block, axis, 0, 0, axis_index_groups=groups)  12.9 us
    ppermute x6, starting transfers between devices, shifted(): lax.ppermute(block, axis, [(s, (s + distance) % count) for s in range(cou...  7.41 us
    ppermute x3, starting transfers between devices, other_core(): return lax.ppermute(block, 'tp', [(s, s ^ 1) for s in range(count)])  5.31 us
    all_to_all x3, waiting for transfers between devices, exchange(): return lax.all_to_all(block, axis, 0, 0, axis_index_groups=groups)  3.99 us
  transfers between devices with their start and end apart: 14, of which 8 were waited for; matrix products, arithmetic and copies ran while one was open for 0% of the time, Pallas kernels for 12%

profile of v3, /device:TPU:1, one launch (start us, length us, event | category | flops | bytes accessed | tf_op | source)
XLA Modules:
  0.0 147.0 jit_solution(6123653348633222030)
XLA Ops:
  6.5 0.0 all-gather.5.cloned.1.call-start
  6.5 2.0 %cut.1 = (bf16[4,80,2048]{2,1,0:T(8,128)(2,1)S(1)}, bf16[160,2048]{1,0:T(8,128)(2,1)}) custom-call(bf16[160,8192]{1,0:T(8,128)(2,1)} %tokens.3, bf16[128,2048]{1,0:T(8,128)(2,1)} %output.1, bf16[32,2048]{1,0:T(8,128)(2,1)} %bitcast.9), custom_call_target="tpu_custom_call" | custom-call | tf_op jit(solution)/shard_map/cut/pallas_call | solution.py:56
  8.5 0.0 all-gather.5.cloned.1.call-update
  8.6 0.0 copy-start.1
  8.6 0.0 copy-start.3
  8.6 20.0 %all_to_all.35.rows = bf16[4,80,2048]{2,1,0:T(8,128)(2,1)S(1)} all-to-all(bf16[4,80,2048]{2,1,0:T(8,128)(2,1)S(1)} %get-tuple-element.23), channel_id=1, replica_groups=mesh['inst'=4,'tp'=8] {'inst'}, dimensions={0} | all-to-all | bytes 2621440 | tf_op jit(solution)/shard_map/all_to_all | solution.py:24
  28.6 2.1 %collective-permute-start = (bf16[4,80,2048]{2,1,0:T(8,128)(2,1)S(1)}, bf16[4,80,2048]{2,1,0:T(8,128)(2,1)S(1)}, u32[]{:S(2)}, u32[]{:S(2)}) collective-permute-start(bf16[4,80,2048]{2,1,0:T(8,128)(2,1)S(1)} %all_to_all.35.rows), channel_id=1, source_target_pairs={{0,1},{1,0},{2,3},{3,2},{4,5},{5,4},{6,7},{7,6},{8,9},{9,8},{10,11... | collective-permute-start | bytes 3932168 | tf_op jit(solution)/shard_map/ppermute | solution.py:29
  30.7 0.0 copy-done.1
  30.7 0.0 copy-done.3
  30.7 0.3 widen.1.weight
  31.0 1.4 project.2
  32.4 1.0 collective-permute-done.rows
  33.3 1.9 %project.3 = (bf16[4,80,2048]{2,1,0:T(8,128)(2,1)}, bf16[4,160,256]{2,1,0:T(8,128)(2,1)}) custom-call(bf16[4,80,2048]{2,1,0:T(8,128)(2,1)S(1)} %collective-permute-done.rows, bf16[2048,256]{1,0:T(8,128)(2,1)S(1)} %widen.1.weight, bf16[4,80,256]{2,1,0:T(8,128)(2,1)S(1)} %get-tuple-element.25.refs_0_), custom_call_target="tpu_custom_call" | custom-call | tf_op jit(solution)/shard_map/project/pallas_call | solution.py:56
  35.3 3.5 %all-to-all-start.1 = ((bf16[4,160,256]{2,1,0:T(8,128)(2,1)}), bf16[4,160,256]{2,1,0:T(8,128)(2,1)S(1)}, u32[]{:S(2)}, u32[]{:S(2)}) async-start(bf16[4,160,256]{2,1,0:T(8,128)(2,1)} %get-tuple-element.27), calls=%async_computation.1 | async-start | bytes 655360 | tf_op jit(solution)/shard_map/all_to_all | solution.py:24
  38.7 0.0 copy-start.2
  38.8 0.0 copy-start.4
  38.8 2.0 %norms.1.scale = f32[160,1]{1,0:T(8,128)S(1)} custom-call(bf16[160,8192]{1,0:T(8,128)(2,1)} %tokens.3), custom_call_target="tpu_custom_call" | custom-call | tf_op jit(solution)/shard_map/norms/pallas_call | solution.py:56
  40.8 3.7 %all-to-all-done.1.parts = bf16[4,160,256]{2,1,0:T(8,128)(2,1)S(1)} async-done(((bf16[4,160,256]{2,1,0:T(8,128)(2,1)}), bf16[4,160,256]{2,1,0:T(8,128)(2,1)S(1)}, u32[]{:S(2)}, u32[]{:S(2)}) %all-to-all-start.1) | async-done | bytes 327712 | tf_op jit(solution)/shard_map/all_to_all | solution.py:24
  44.5 0.9 finish.1
  45.4 6.0 %all-to-all-start.2 = ((bf16[8,32,160]{2,1,0:T(8,128)(2,1)}), bf16[8,32,160]{2,1,0:T(8,128)(2,1)S(1)}, u32[]{:S(2)}, u32[]{:S(2)}) async-start(bf16[8,32,160]{2,1,0:T(8,128)(2,1)} %get-tuple-element.29), calls=%async_computation.2 | async-start | bytes 262144 | tf_op jit(solution)/shard_map/all_to_all | solution.py:24
  51.3 0.0 copy-done.2
  51.4 1.2 collective-permute-start.1
  52.6 0.3 collective-permute-start.2
  52.9 2.1 %collective-permute-start.3 = (bf16[32,2048]{1,0:T(8,128)(2,1)S(1)}, bf16[32,2048]{1,0:T(8,128)(2,1)S(1)}, u32[]{:S(2)}, u32[]{:S(2)}) collective-permute-start(bf16[32,2048]{1,0:T(8,128)(2,1)S(1)} %get-tuple-element.33), channel_id=1, source_target_pairs={{0,24},{8,0},{16,8},{24,16},{1,25},{9,1},{17,9},{25,17},{2,26},{10... | collective-permute-start | bytes 393224 | tf_op jit(solution)/shard_map/ppermute | solution.py:73
  55.0 2.6 %collective-permute-done.1.refs_1_ = bf16[32,2048]{1,0:T(8,128)(2,1)S(1)} collective-permute-done((bf16[32,2048]{1,0:T(8,128)(2,1)S(1)}, bf16[32,2048]{1,0:T(8,128)(2,1)S(1)}, u32[]{:S(2)}, u32[]{:S(2)}) %collective-permute-start.1) | collective-permute-done | bytes 131104 | tf_op jit(solution)/shard_map/ppermute | solution.py:73
  57.6 3.1 %collective-permute-done.2.refs_2_ = bf16[32,2048]{1,0:T(8,128)(2,1)S(1)} collective-permute-done((bf16[32,2048]{1,0:T(8,128)(2,1)S(1)}, bf16[32,2048]{1,0:T(8,128)(2,1)S(1)}, u32[]{:S(2)}, u32[]{:S(2)}) %collective-permute-start.2) | collective-permute-done | bytes 131104 | tf_op jit(solution)/shard_map/ppermute | solution.py:73
  60.7 0.0 collective-permute-done.3.refs_3_
  60.7 0.3 all-to-all-done.2.pieces
  61.0 0.0 copy-done.4
  61.0 0.5 attend.2
  61.5 9.5 %all_to_all.36.heads = bf16[4,160,128]{2,1,0:T(8,128)(2,1)S(1)} all-to-all(bf16[4,160,128]{2,1,0:T(8,128)(2,1)S(1)} %attend.2), channel_id=1, replica_groups={{0,2,4,6},{1,3,5,7},{8,10,12,14},{9,11,13,15},{16,18,20,22},{17,19,21,2..., dimensions={0} | all-to-all | bytes 327680 | tf_op jit(solution)/shard_map/all_to_all | solution.py:24
  71.0 0.9 spread.1
  71.9 3.5 %all-to-all-start.4 = ((bf16[4,4,160,128]{3,2,1,0:T(8,128)(2,1)}), bf16[4,4,160,128]{3,2,1,0:T(8,128)(2,1)S(1)}, u32[]{:S(2)}, u32[]{:S(2)}) async-start(bf16[4,4,160,128]{3,2,1,0:T(8,128)(2,1)} %spread.1), calls=%async_computation.4 | async-start | bytes 1310720 | tf_op jit(solution)/shard_map/all_to_all | solution.py:24
  75.4 0.0 all-gather.7.cloned.1.call-start
  75.4 0.1 aim.1
  75.5 0.6 collective-permute-start.4
  76.2 2.2 %collective-permute-start.5 = (bf16[32,2048]{1,0:T(8,128)(2,1)S(1)}, bf16[32,2048]{1,0:T(8,128)(2,1)S(1)}, u32[]{:S(2)}, u32[]{:S(2)}) collective-permute-start(bf16[32,2048]{1,0:T(8,128)(2,1)S(1)} %get-tuple-element.37), channel_id=1, source_target_pairs={{0,4},{1,5},{2,6},{3,7},{4,0},{5,1},{6,2},{7,3},{8,12},{9,13},{10,... | collective-permute-start | bytes 393224 | tf_op jit(solution)/shard_map/ppermute | solution.py:73
  78.3 1.0 collective-permute-start.6
  79.3 2.0 %collective-permute-done.4.refs_1_ = bf16[32,2048]{1,0:T(8,128)(2,1)S(1)} collective-permute-done((bf16[32,2048]{1,0:T(8,128)(2,1)S(1)}, bf16[32,2048]{1,0:T(8,128)(2,1)S(1)}, u32[]{:S(2)}, u32[]{:S(2)}) %collective-permute-start.4) | collective-permute-done | bytes 131104 | tf_op jit(solution)/shard_map/ppermute | solution.py:73
  81.4 6.4 %collective-permute-done.5.refs_2_ = bf16[32,2048]{1,0:T(8,128)(2,1)S(1)} collective-permute-done((bf16[32,2048]{1,0:T(8,128)(2,1)S(1)}, bf16[32,2048]{1,0:T(8,128)(2,1)S(1)}, u32[]{:S(2)}, u32[]{:S(2)}) %collective-permute-start.5) | collective-permute-done | bytes 131104 | tf_op jit(solution)/shard_map/ppermute | solution.py:73
  87.8 0.0 collective-permute-done.6.refs_3_
  87.8 0.0 all-to-all-done.4.source
  87.8 0.0 all-gather.5.cloned.1.call-done
  87.8 0.0 copy-start
  87.8 0.9 keep.1
  88.7 0.0 all-gather.7.cloned.1.call-update
  88.7 1.4 collective-permute-start.7
  90.2 1.7 %collective-permute-done.7.other = bf16[4,4,160,128]{3,2,1,0:T(8,128)(2,1)S(1)} collective-permute-done((bf16[4,4,160,128]{3,2,1,0:T(8,128)(2,1)S(1)}, bf16[4,4,160,128]{3,2,1,0:T(8,128)(2,1)S(1)}, u32[]{:S(2)}, u32[]{:S(2)}) %collective-permute-start.7) | collective-permute-done | bytes 655392 | tf_op jit(solution)/shard_map/ppermute | solution.py:29
  91.9 0.0 copy-done
  91.9 6.9 %advance.1 = bf16[4,176,640]{2,1,0:T(8,128)(2,1)S(1)} custom-call(bf16[4,80,2048]{2,1,0:T(8,128)(2,1)} %get-tuple-element.24.own_rows, bf16[4,80,2048]{2,1,0:T(8,128)(2,1)} %get-tuple-element.26.other_rows, bf16[4,4,160,128]{3,2,1,0:T(8,128)(2,1)S(1)} %get-tuple-element.39.mine, bf16[4,4,160,128]{3,2,1,0:T(8,128)(2,1)S(1)} %collective-permute-done.7.other, ...), custom_call_target="tpu_custom_call" | custom-call | tf_op jit(solution)/shard_map/advance/pallas_call | solution.py:56
  98.8 17.6 %all_to_all.37.parts = bf16[4,176,640]{2,1,0:T(8,128)(2,1)S(1)} all-to-all(bf16[4,176,640]{2,1,0:T(8,128)(2,1)S(1)} %advance.1), channel_id=1, replica_groups=mesh['inst'=4,'tp'=8] {'inst'}, dimensions={0} | all-to-all | bytes 1802240 | tf_op jit(solution)/shard_map/all_to_all | solution.py:24
  116.4 0.6 attend.3
  117.0 17.1 %all_to_all.38.got = bf16[4,160,384]{2,1,0:T(8,128)(2,1)S(1)} all-to-all(bf16[4,160,384]{2,1,0:T(8,128)(2,1)S(1)} %attend.3), channel_id=1, replica_groups={{0,2,4,6},{1,3,5,7},{8,10,12,14},{9,11,13,15},{16,18,20,22},{17,19,21,2..., dimensions={0} | all-to-all | bytes 983040 | tf_op jit(solution)/shard_map/all_to_all | solution.py:24
  134.1 0.0 all-gather.7.cloned.1.call-done
  134.1 1.7 %blend.3 = bf16[160,1024]{1,0:T(8,128)(2,1)S(1)} custom-call(bf16[4,160,384]{2,1,0:T(8,128)(2,1)S(1)} %all_to_all.38.got, bf16[4,4,32,2048]{3,2,1,0:T(8,128)(2,1)} %bitcast.7), custom_call_target="tpu_custom_call" | custom-call | tf_op jit(solution)/shard_map/blend/pallas_call | solution.py:56
  135.9 1.8 %collective-permute-start.8 = (bf16[160,1024]{1,0:T(8,128)(2,1)S(1)}, bf16[160,1024]{1,0:T(8,128)(2,1)S(1)}, u32[]{:S(2)}, u32[]{:S(2)}) collective-permute-start(bf16[160,1024]{1,0:T(8,128)(2,1)S(1)} %blend.3), channel_id=1, source_target_pairs={{0,1},{1,0},{2,3},{3,2},{4,5},{5,4},{6,7},{7,6},{8,9},{9,8},{10,11... | collective-permute-start | bytes 983048 | tf_op jit(solution)/shard_map/ppermute | solution.py:29
  137.7 1.7 %blend.2.kept = f32[160,1024]{1,0:T(8,128)S(1)} custom-call(bf16[4,160,384]{2,1,0:T(8,128)(2,1)S(1)} %all_to_all.38.got, bf16[4,4,32,2048]{3,2,1,0:T(8,128)(2,1)} %bitcast.8), custom_call_target="tpu_custom_call" | custom-call | tf_op jit(solution)/shard_map/blend/pallas_call | solution.py:56
  139.4 0.0 collective-permute-done.8.arrived
  139.4 0.8 join.1
  (1 shorter events, 0.0 us)
Async XLA Ops:
  6.5 81.2 %all-gather.5.cloned.1.call-start = ((), (), s32[]{:S(2)}) async-start(), calls=%async_computation.7 | async-start | bytes 5898240 | tf_op jit(solution)/shard_map/all_gather | solution.py:473
  8.6 22.1 %copy-start.1 = (bf16[2048,128]{1,0:T(8,128)(2,1)S(1)}, bf16[2048,128]{1,0:T(8,128)(2,1)}, u32[]{:S(2)}) copy-start(bf16[2048,128]{1,0:T(8,128)(2,1)} %query.2) | copy-start | bytes 1572868
  8.6 22.1 %copy-start.3 = (bf16[2048,32]{0,1:T(8,128)(2,1)S(1)}, bf16[2048,32]{0,1:T(8,128)(2,1)}, u32[]{:S(2)}) copy-start(bf16[2048,32]{0,1:T(8,128)(2,1)} %param.11) | copy-start | bytes 393220
  28.6 4.8 %collective-permute-start = (bf16[4,80,2048]{2,1,0:T(8,128)(2,1)S(1)}, bf16[4,80,2048]{2,1,0:T(8,128)(2,1)S(1)}, u32[]{:S(2)}, u32[]{:S(2)}) collective-permute-start(bf16[4,80,2048]{2,1,0:T(8,128)(2,1)S(1)} %all_to_all.35.rows), channel_id=1, source_target_pairs={{0,1},{1,0},{2,3},{3,2},{4,5},{5,4},{6,7},{7,6},{8,9},{9,8},{10,11... | collective-permute-start | bytes 3932168 | tf_op jit(solution)/shard_map/ppermute | solution.py:29
  35.3 9.2 %all-to-all-start.1 = ((bf16[4,160,256]{2,1,0:T(8,128)(2,1)}), bf16[4,160,256]{2,1,0:T(8,128)(2,1)S(1)}, u32[]{:S(2)}, u32[]{:S(2)}) async-start(bf16[4,160,256]{2,1,0:T(8,128)(2,1)} %get-tuple-element.27), calls=%async_computation.1 | async-start | bytes 655360 | tf_op jit(solution)/shard_map/all_to_all | solution.py:24
  38.7 12.6 %copy-start.2 = (bf16[128,2048]{1,0:T(8,128)(2,1)S(1)}, bf16[128,2048]{1,0:T(8,128)(2,1)}, u32[]{:S(2)}) copy-start(bf16[128,2048]{1,0:T(8,128)(2,1)} %shard.1) | copy-start | bytes 1572868
  38.8 22.2 %copy-start.4 = (s32[4,160]{1,0:T(4,128)S(1)}, s32[4,160]{1,0:T(4,128)}, u32[]{:S(2)}) copy-start(s32[4,160]{1,0:T(4,128)} %doc_ids.3) | copy-start | bytes 7684
  45.4 15.6 %all-to-all-start.2 = ((bf16[8,32,160]{2,1,0:T(8,128)(2,1)}), bf16[8,32,160]{2,1,0:T(8,128)(2,1)S(1)}, u32[]{:S(2)}, u32[]{:S(2)}) async-start(bf16[8,32,160]{2,1,0:T(8,128)(2,1)} %get-tuple-element.29), calls=%async_computation.2 | async-start | bytes 262144 | tf_op jit(solution)/shard_map/all_to_all | solution.py:24
  51.4 6.2 %collective-permute-start.1 = (bf16[32,2048]{1,0:T(8,128)(2,1)S(1)}, bf16[32,2048]{1,0:T(8,128)(2,1)S(1)}, u32[]{:S(2)}, u32[]{:S(2)}) collective-permute-start(bf16[32,2048]{1,0:T(8,128)(2,1)S(1)} %get-tuple-element.31), channel_id=1, source_target_pairs={{0,8},{8,16},{16,24},{24,0},{1,9},{9,17},{17,25},{25,1},{2,10},{10... | collective-permute-start | bytes 393224 | tf_op jit(solution)/shard_map/ppermute | solution.py:73
  52.6 8.1 %collective-permute-start.2 = (bf16[32,2048]{1,0:T(8,128)(2,1)S(1)}, bf16[32,2048]{1,0:T(8,128)(2,1)S(1)}, u32[]{:S(2)}, u32[]{:S(2)}) collective-permute-start(bf16[32,2048]{1,0:T(8,128)(2,1)S(1)} %get-tuple-element.32), channel_id=1, source_target_pairs={{0,16},{8,24},{16,0},{24,8},{1,17},{9,25},{17,1},{25,9},{2,18},{10... | collective-permute-start | bytes 393224 | tf_op jit(solution)/shard_map/ppermute | solution.py:73
  52.9 7.8 %collective-permute-start.3 = (bf16[32,2048]{1,0:T(8,128)(2,1)S(1)}, bf16[32,2048]{1,0:T(8,128)(2,1)S(1)}, u32[]{:S(2)}, u32[]{:S(2)}) collective-permute-start(bf16[32,2048]{1,0:T(8,128)(2,1)S(1)} %get-tuple-element.33), channel_id=1, source_target_pairs={{0,24},{8,0},{16,8},{24,16},{1,25},{9,1},{17,9},{25,17},{2,26},{10... | collective-permute-start | bytes 393224 | tf_op jit(solution)/shard_map/ppermute | solution.py:73
  71.9 15.9 %all-to-all-start.4 = ((bf16[4,4,160,128]{3,2,1,0:T(8,128)(2,1)}), bf16[4,4,160,128]{3,2,1,0:T(8,128)(2,1)S(1)}, u32[]{:S(2)}, u32[]{:S(2)}) async-start(bf16[4,4,160,128]{3,2,1,0:T(8,128)(2,1)} %spread.1), calls=%async_computation.4 | async-start | bytes 1310720 | tf_op jit(solution)/shard_map/all_to_all | solution.py:24
  75.4 58.8 %all-gather.7.cloned.1.call-start = ((), (), s32[]{:S(2)}) async-start(), calls=%async_computation.8 | async-start | bytes 2621440 | tf_op jit(solution)/shard_map/all_gather | solution.py:487
  75.5 5.8 %collective-permute-start.4 = (bf16[32,2048]{1,0:T(8,128)(2,1)S(1)}, bf16[32,2048]{1,0:T(8,128)(2,1)S(1)}, u32[]{:S(2)}, u32[]{:S(2)}) collective-permute-start(bf16[32,2048]{1,0:T(8,128)(2,1)S(1)} %get-tuple-element.36), channel_id=1, source_target_pairs={{0,2},{1,3},{2,4},{3,5},{4,6},{5,7},{6,0},{7,1},{8,10},{9,11},{10,... | collective-permute-start | bytes 393224 | tf_op jit(solution)/shard_map/ppermute | solution.py:73
  76.2 11.6 %collective-permute-start.5 = (bf16[32,2048]{1,0:T(8,128)(2,1)S(1)}, bf16[32,2048]{1,0:T(8,128)(2,1)S(1)}, u32[]{:S(2)}, u32[]{:S(2)}) collective-permute-start(bf16[32,2048]{1,0:T(8,128)(2,1)S(1)} %get-tuple-element.37), channel_id=1, source_target_pairs={{0,4},{1,5},{2,6},{3,7},{4,0},{5,1},{6,2},{7,3},{8,12},{9,13},{10,... | collective-permute-start | bytes 393224 | tf_op jit(solution)/shard_map/ppermute | solution.py:73
  78.3 9.4 %collective-permute-start.6 = (bf16[32,2048]{1,0:T(8,128)(2,1)S(1)}, bf16[32,2048]{1,0:T(8,128)(2,1)S(1)}, u32[]{:S(2)}, u32[]{:S(2)}) collective-permute-start(bf16[32,2048]{1,0:T(8,128)(2,1)S(1)} %get-tuple-element.38), channel_id=1, source_target_pairs={{0,6},{1,7},{2,0},{3,1},{4,2},{5,3},{6,4},{7,5},{8,14},{9,15},{10,... | collective-permute-start | bytes 393224 | tf_op jit(solution)/shard_map/ppermute | solution.py:73
  87.8 4.1 %copy-start = (bf16[2048,128]{1,0:T(8,128)(2,1)S(1)}, bf16[2048,128]{1,0:T(8,128)(2,1)}, u32[]{:S(2)}) copy-start(bf16[2048,128]{1,0:T(8,128)(2,1)} %query.3) | copy-start | bytes 1572868
  88.7 3.1 %collective-permute-start.7 = (bf16[4,4,160,128]{3,2,1,0:T(8,128)(2,1)S(1)}, bf16[4,4,160,128]{3,2,1,0:T(8,128)(2,1)S(1)}, u32[]{:S(2)}, u32[]{:S(2)}) collective-permute-start(bf16[4,4,160,128]{3,2,1,0:T(8,128)(2,1)S(1)} %get-tuple-element.39.mine), channel_id=1, source_target_pairs={{0,1},{1,0},{2,3},{3,2},{4,5},{5,4},{6,7},{7,6},{8,9},{9,8},{10,11... | collective-permute-start | bytes 1966088 | tf_op jit(solution)/shard_map/ppermute | solution.py:29
  135.9 3.5 %collective-permute-start.8 = (bf16[160,1024]{1,0:T(8,128)(2,1)S(1)}, bf16[160,1024]{1,0:T(8,128)(2,1)S(1)}, u32[]{:S(2)}, u32[]{:S(2)}) collective-permute-start(bf16[160,1024]{1,0:T(8,128)(2,1)S(1)} %blend.3), channel_id=1, source_target_pairs={{0,1},{1,0},{2,3},{3,2},{4,5},{5,4},{6,7},{7,6},{8,9},{9,8},{10,11... | collective-permute-start | bytes 983048 | tf_op jit(solution)/shard_map/ppermute | solution.py:29
Sparse Core Ops, SparseCore 0:
  9.0 61.3 all-gather.4
  88.9 42.0 all-gather.6

commit v4 on v3

--- a/solution.py
+++ b/solution.py
@@ -182,17 +182,15 @@
     return call(kernel, "aim", [bfloat(*shape)] * planes, [VMEM] * len(arrived), arrived, scratch)
 
 
-def keep_kernel(source, output, *refs):
-    pieces, (kept, rows) = refs[:-2], refs[-2:]
-    kept[...] = source[...]
-    for e, piece in enumerate(pieces):
-        rows[e] = piece[...]
-
-
-def keep(block, output, pieces):
-    outs = [bfloat(*block.shape), bfloat(len(pieces), *pieces[0].shape)]
-    ins = [VMEM, HBM] + [VMEM] * len(pieces)
-    return call(keep_kernel, "keep", outs, ins, [block, output, *pieces], places=[VMEM, LAST])
+def stack_kernel(*refs):
+    for e, piece in enumerate(refs[:-2]):
+        refs[-1][e] = piece[...]
+
+
+def stacked(pieces, block):
+    args = [*pieces, block]
+    outs = [bfloat(len(pieces), *pieces[0].shape)]
+    return call(stack_kernel, "stack", outs, [VMEM] * len(args), args, places=[LAST])[0]
 
 
 def project_kernel(rows, weight, *refs):
@@ -300,14 +298,14 @@
     return call(kernel, "attend", outs, [VMEM] * 2, [parts, doc_ids])[0]
 
 
-def spread_kernel(heads, sent):
+def spread_kernel(heads, output, sent):
     for q in range(sent.shape[0]):
         sent[q] = heads[...]
 
 
-def spread(heads):
+def spread(heads, output):
     outs = [bfloat(lax.axis_size("inst"), *heads.shape)]
-    return call(spread_kernel, "spread", outs, [VMEM], [heads])[0]
+    return call(spread_kernel, "spread", outs, [VMEM, HBM], [heads, output])[0]
 
 
 def spans(count):
@@ -482,7 +480,8 @@
     pieces = [pieces[0]] + [shifted(pieces[e], "tp", 2 * e) for e in range(1, ranks // 2)]
     context = first_attend(queries, doc_ids, exchange(keyvals_t, "tp", groups), arrived)
     heads = exchange(context, "tp", core_groups())
-    mine, rows_by = keep(exchange(spread(heads), "inst"), output_all, pieces)
+    mine = exchange(spread(heads, output_all), "inst")
+    rows_by = stacked(pieces, mine)
     sums = advance(own_rows, other_rows, mine, other_core(mine), output_all, query_two, rows_by)
     rows_by = lax.all_gather(rows_by, "inst", axis=0)
 

time: 148 us -> 148 us (level)
  starting transfers between devices: 25.7 us -> 27.6 us
  transfers between devices with their start and end apart: 14 -> 14, of which waited for: 8 -> 9; matrix products, arithmetic and copies ran while one was open for 0% -> 0% of each run, Pallas kernels for 12% -> 11%
where the time goes in v4:
time: 148 us; the launch traced here: 147 us
  blocking collectives  63.3 us (43%)
  starting transfers between devices  27.6 us (19%)
  Pallas kernels  22.6 us (15%)
  waiting for transfers between devices  19.9 us (13%)
  between operations  13.6 us (9%)
    all_to_all x4, blocking collectives, exchange(): return lax.all_to_all(block, axis, 0, 0, axis_index_groups=groups)  63.3 us
    pallas_call x16, Pallas kernels, call(): pl.pallas_call(kernel, out_shape=outs, in_specs=ins, out_specs=[VMEM if s...  22.6 us
    all_to_all x3, starting transfers between devices, exchange(): return lax.all_to_all(block, axis, 0, 0, axis_index_groups=groups)  14 us
    ppermute x6, waiting for transfers between devices, shifted(): lax.ppermute(block, axis, [(s, (s + distance) % count) for s in range(cou...  13.2 us
    ppermute x6, starting transfers between devices, shifted(): lax.ppermute(block, axis, [(s, (s + distance) % count) for s in range(cou...  6.91 us
    ppermute x3, starting transfers between devices, other_core(): return lax.ppermute(block, 'tp', [(s, s ^ 1) for s in range(count)])  6.72 us
    all_to_all x3, waiting for transfers between devices, exchange(): return lax.all_to_all(block, axis, 0, 0, axis_index_groups=groups)  3.98 us
  transfers between devices with their start and end apart: 14, of which 9 were waited for; matrix products, arithmetic and copies ran while one was open for 0% of the time, Pallas kernels for 11%

profile of v4, /device:TPU:1, one launch (start us, length us, event | category | flops | bytes accessed | tf_op | source)
XLA Modules:
  0.0 146.9 jit_solution(3656925879999999051)
XLA Ops:
  6.5 0.0 all-gather.5.cloned.1.call-start
  6.5 2.0 %cut.1 = (bf16[4,80,2048]{2,1,0:T(8,128)(2,1)S(1)}, bf16[160,2048]{1,0:T(8,128)(2,1)}) custom-call(bf16[160,8192]{1,0:T(8,128)(2,1)} %tokens.3, bf16[128,2048]{1,0:T(8,128)(2,1)} %output.1, bf16[32,2048]{1,0:T(8,128)(2,1)} %bitcast.9), custom_call_target="tpu_custom_call" | custom-call | tf_op jit(solution)/shard_map/cut/pallas_call | solution.py:56
  8.5 0.0 all-gather.5.cloned.1.call-update
  8.5 0.0 copy-start.1
  8.5 0.0 copy-start.3
  8.6 20.0 %all_to_all.35.rows = bf16[4,80,2048]{2,1,0:T(8,128)(2,1)S(1)} all-to-all(bf16[4,80,2048]{2,1,0:T(8,128)(2,1)S(1)} %get-tuple-element.21), channel_id=1, replica_groups=mesh['inst'=4,'tp'=8] {'inst'}, dimensions={0} | all-to-all | bytes 2621440 | tf_op jit(solution)/shard_map/all_to_all | solution.py:24
  28.6 2.1 %collective-permute-start = (bf16[4,80,2048]{2,1,0:T(8,128)(2,1)S(1)}, bf16[4,80,2048]{2,1,0:T(8,128)(2,1)S(1)}, u32[]{:S(2)}, u32[]{:S(2)}) collective-permute-start(bf16[4,80,2048]{2,1,0:T(8,128)(2,1)S(1)} %all_to_all.35.rows), channel_id=1, source_target_pairs={{0,1},{1,0},{2,3},{3,2},{4,5},{5,4},{6,7},{7,6},{8,9},{9,8},{10,11... | collective-permute-start | bytes 3932168 | tf_op jit(solution)/shard_map/ppermute | solution.py:29
  30.7 0.0 copy-done.1
  30.7 0.0 copy-done.3
  30.7 0.3 widen.1.weight
  31.0 1.4 project.2
  32.4 0.9 collective-permute-done.rows
  33.3 1.9 %project.3 = (bf16[4,80,2048]{2,1,0:T(8,128)(2,1)}, bf16[4,160,256]{2,1,0:T(8,128)(2,1)}) custom-call(bf16[4,80,2048]{2,1,0:T(8,128)(2,1)S(1)} %collective-permute-done.rows, bf16[2048,256]{1,0:T(8,128)(2,1)S(1)} %widen.1.weight, bf16[4,80,256]{2,1,0:T(8,128)(2,1)S(1)} %get-tuple-element.23.refs_0_), custom_call_target="tpu_custom_call" | custom-call | tf_op jit(solution)/shard_map/project/pallas_call | solution.py:56
  35.3 3.5 %all-to-all-start.1 = ((bf16[4,160,256]{2,1,0:T(8,128)(2,1)}), bf16[4,160,256]{2,1,0:T(8,128)(2,1)S(1)}, u32[]{:S(2)}, u32[]{:S(2)}) async-start(bf16[4,160,256]{2,1,0:T(8,128)(2,1)} %get-tuple-element.25), calls=%async_computation.1 | async-start | bytes 655360 | tf_op jit(solution)/shard_map/all_to_all | solution.py:24
  38.7 0.0 copy-start.2
  38.7 0.0 copy-start.4
  38.8 2.0 %norms.1.scale = f32[160,1]{1,0:T(8,128)S(1)} custom-call(bf16[160,8192]{1,0:T(8,128)(2,1)} %tokens.3), custom_call_target="tpu_custom_call" | custom-call | tf_op jit(solution)/shard_map/norms/pallas_call | solution.py:56
  40.8 3.7 %all-to-all-done.1.parts = bf16[4,160,256]{2,1,0:T(8,128)(2,1)S(1)} async-done(((bf16[4,160,256]{2,1,0:T(8,128)(2,1)}), bf16[4,160,256]{2,1,0:T(8,128)(2,1)S(1)}, u32[]{:S(2)}, u32[]{:S(2)}) %all-to-all-start.1) | async-done | bytes 327712 | tf_op jit(solution)/shard_map/all_to_all | solution.py:24
  44.4 0.9 finish.1
  45.3 6.0 %all-to-all-start.2 = ((bf16[8,32,160]{2,1,0:T(8,128)(2,1)}), bf16[8,32,160]{2,1,0:T(8,128)(2,1)S(1)}, u32[]{:S(2)}, u32[]{:S(2)}) async-start(bf16[8,32,160]{2,1,0:T(8,128)(2,1)} %get-tuple-element.27), calls=%async_computation.2 | async-start | bytes 262144 | tf_op jit(solution)/shard_map/all_to_all | solution.py:24
  51.3 0.0 copy-done.2
  51.4 1.2 collective-permute-start.1
  52.6 0.3 collective-permute-start.2
  52.8 2.1 %collective-permute-start.3 = (bf16[32,2048]{1,0:T(8,128)(2,1)S(1)}, bf16[32,2048]{1,0:T(8,128)(2,1)S(1)}, u32[]{:S(2)}, u32[]{:S(2)}) collective-permute-start(bf16[32,2048]{1,0:T(8,128)(2,1)S(1)} %get-tuple-element.31), channel_id=1, source_target_pairs={{0,24},{8,0},{16,8},{24,16},{1,25},{9,1},{17,9},{25,17},{2,26},{10... | collective-permute-start | bytes 393224 | tf_op jit(solution)/shard_map/ppermute | solution.py:73
  55.0 2.6 %collective-permute-done.1.refs_1_ = bf16[32,2048]{1,0:T(8,128)(2,1)S(1)} collective-permute-done((bf16[32,2048]{1,0:T(8,128)(2,1)S(1)}, bf16[32,2048]{1,0:T(8,128)(2,1)S(1)}, u32[]{:S(2)}, u32[]{:S(2)}) %collective-permute-start.1) | collective-permute-done | bytes 131104 | tf_op jit(solution)/shard_map/ppermute | solution.py:73
  57.6 3.1 %collective-permute-done.2.refs_2_ = bf16[32,2048]{1,0:T(8,128)(2,1)S(1)} collective-permute-done((bf16[32,2048]{1,0:T(8,128)(2,1)S(1)}, bf16[32,2048]{1,0:T(8,128)(2,1)S(1)}, u32[]{:S(2)}, u32[]{:S(2)}) %collective-permute-start.2) | collective-permute-done | bytes 131104 | tf_op jit(solution)/shard_map/ppermute | solution.py:73
  60.7 0.0 collective-permute-done.3.refs_3_
  60.7 0.3 all-to-all-done.2.pieces
  61.0 0.0 copy-done.4
  61.0 0.5 attend.2
  61.4 9.5 %all_to_all.36.heads = bf16[4,160,128]{2,1,0:T(8,128)(2,1)S(1)} all-to-all(bf16[4,160,128]{2,1,0:T(8,128)(2,1)S(1)} %attend.2), channel_id=1, replica_groups={{0,2,4,6},{1,3,5,7},{8,10,12,14},{9,11,13,15},{16,18,20,22},{17,19,21,2..., dimensions={0} | all-to-all | bytes 327680 | tf_op jit(solution)/shard_map/all_to_all | solution.py:24
  71.0 0.0 all-gather.5.cloned.1.call-done
  71.0 0.9 spread.1
  71.9 4.6 %all-to-all-start.4 = ((bf16[4,4,160,128]{3,2,1,0:T(8,128)(2,1)}), bf16[4,4,160,128]{3,2,1,0:T(8,128)(2,1)S(1)}, u32[]{:S(2)}, u32[]{:S(2)}) async-start(bf16[4,4,160,128]{3,2,1,0:T(8,128)(2,1)} %spread.1), calls=%async_computation.4 | async-start | bytes 1310720 | tf_op jit(solution)/shard_map/all_to_all | solution.py:24
  76.4 0.0 copy-start
  76.4 0.0 all-gather.7.cloned.1.call-start
  76.4 0.1 aim.1
  76.5 0.1 collective-permute-start.5
  76.6 1.7 %collective-permute-start.6 = (bf16[32,2048]{1,0:T(8,128)(2,1)S(1)}, bf16[32,2048]{1,0:T(8,128)(2,1)S(1)}, u32[]{:S(2)}, u32[]{:S(2)}) collective-permute-start(bf16[32,2048]{1,0:T(8,128)(2,1)S(1)} %get-tuple-element.35), channel_id=1, source_target_pairs={{0,4},{1,5},{2,6},{3,7},{4,0},{5,1},{6,2},{7,3},{8,12},{9,13},{10,... | collective-permute-start | bytes 393224 | tf_op jit(solution)/shard_map/ppermute | solution.py:73
  78.3 1.5 %collective-permute-start.7 = (bf16[32,2048]{1,0:T(8,128)(2,1)S(1)}, bf16[32,2048]{1,0:T(8,128)(2,1)S(1)}, u32[]{:S(2)}, u32[]{:S(2)}) collective-permute-start(bf16[32,2048]{1,0:T(8,128)(2,1)S(1)} %get-tuple-element.36), channel_id=1, source_target_pairs={{0,6},{1,7},{2,0},{3,1},{4,2},{5,3},{6,4},{7,5},{8,14},{9,15},{10,... | collective-permute-start | bytes 393224 | tf_op jit(solution)/shard_map/ppermute | solution.py:73
  79.8 2.6 %collective-permute-done.5.refs_1_ = bf16[32,2048]{1,0:T(8,128)(2,1)S(1)} collective-permute-done((bf16[32,2048]{1,0:T(8,128)(2,1)S(1)}, bf16[32,2048]{1,0:T(8,128)(2,1)S(1)}, u32[]{:S(2)}, u32[]{:S(2)}) %collective-permute-start.5) | collective-permute-done | bytes 131104 | tf_op jit(solution)/shard_map/ppermute | solution.py:73
  82.4 4.7 %collective-permute-done.6.refs_2_ = bf16[32,2048]{1,0:T(8,128)(2,1)S(1)} collective-permute-done((bf16[32,2048]{1,0:T(8,128)(2,1)S(1)}, bf16[32,2048]{1,0:T(8,128)(2,1)S(1)}, u32[]{:S(2)}, u32[]{:S(2)}) %collective-permute-start.6) | collective-permute-done | bytes 131104 | tf_op jit(solution)/shard_map/ppermute | solution.py:73
  87.1 0.2 collective-permute-done.7.refs_3_
  87.3 0.0 all-to-all-done.4.refs_4_.mine
  87.3 0.9 stack.1.rows_by
  88.2 0.0 all-gather.7.cloned.1.call-update
  88.2 2.8 %collective-permute-start.4 = (bf16[4,4,160,128]{3,2,1,0:T(8,128)(2,1)S(1)}, bf16[4,4,160,128]{3,2,1,0:T(8,128)(2,1)S(1)}, u32[]{:S(2)}, u32[]{:S(2)}) collective-permute-start(bf16[4,4,160,128]{3,2,1,0:T(8,128)(2,1)S(1)} %all-to-all-done.4.refs_4_.mine), channel_id=1, source_target_pairs={{0,1},{1,0},{2,3},{3,2},{4,5},{5,4},{6,7},{7,6},{8,9},{9,8},{10,11... | collective-permute-start | bytes 1966088 | tf_op jit(solution)/shard_map/ppermute | solution.py:29
  91.0 1.7 %collective-permute-done.4.other = bf16[4,4,160,128]{3,2,1,0:T(8,128)(2,1)S(1)} collective-permute-done((bf16[4,4,160,128]{3,2,1,0:T(8,128)(2,1)S(1)}, bf16[4,4,160,128]{3,2,1,0:T(8,128)(2,1)S(1)}, u32[]{:S(2)}, u32[]{:S(2)}) %collective-permute-start.4) | collective-permute-done | bytes 655392 | tf_op jit(solution)/shard_map/ppermute | solution.py:29
  92.8 0.0 copy-done
  92.8 6.9 %advance.1 = bf16[4,176,640]{2,1,0:T(8,128)(2,1)S(1)} custom-call(bf16[4,80,2048]{2,1,0:T(8,128)(2,1)} %get-tuple-element.22.own_rows, bf16[4,80,2048]{2,1,0:T(8,128)(2,1)} %get-tuple-element.24.other_rows, bf16[4,4,160,128]{3,2,1,0:T(8,128)(2,1)S(1)} %all-to-all-done.4.refs_4_.mine, bf16[4,4,160,128]{3,2,1,0:T(8,128)(2,1)S(1)} %collective-permute-done.4.other, ...), custom_call_target="tpu_custom_call" | custom-call | tf_op jit(solution)/shard_map/advance/pallas_call | solution.py:56
  99.7 16.6 %all_to_all.37.parts = bf16[4,176,640]{2,1,0:T(8,128)(2,1)S(1)} all-to-all(bf16[4,176,640]{2,1,0:T(8,128)(2,1)S(1)} %advance.1), channel_id=1, replica_groups=mesh['inst'=4,'tp'=8] {'inst'}, dimensions={0} | all-to-all | bytes 1802240 | tf_op jit(solution)/shard_map/all_to_all | solution.py:24
  116.3 0.6 attend.3
  116.9 17.1 %all_to_all.38.got = bf16[4,160,384]{2,1,0:T(8,128)(2,1)S(1)} all-to-all(bf16[4,160,384]{2,1,0:T(8,128)(2,1)S(1)} %attend.3), channel_id=1, replica_groups={{0,2,4,6},{1,3,5,7},{8,10,12,14},{9,11,13,15},{16,18,20,22},{17,19,21,2..., dimensions={0} | all-to-all | bytes 983040 | tf_op jit(solution)/shard_map/all_to_all | solution.py:24
  134.1 0.0 all-gather.7.cloned.1.call-done
  134.1 1.7 %blend.3 = bf16[160,1024]{1,0:T(8,128)(2,1)S(1)} custom-call(bf16[4,160,384]{2,1,0:T(8,128)(2,1)S(1)} %all_to_all.38.got, bf16[4,4,32,2048]{3,2,1,0:T(8,128)(2,1)} %bitcast.7), custom_call_target="tpu_custom_call" | custom-call | tf_op jit(solution)/shard_map/blend/pallas_call | solution.py:56
  135.8 1.8 %collective-permute-start.8 = (bf16[160,1024]{1,0:T(8,128)(2,1)S(1)}, bf16[160,1024]{1,0:T(8,128)(2,1)S(1)}, u32[]{:S(2)}, u32[]{:S(2)}) collective-permute-start(bf16[160,1024]{1,0:T(8,128)(2,1)S(1)} %blend.3), channel_id=1, source_target_pairs={{0,1},{1,0},{2,3},{3,2},{4,5},{5,4},{6,7},{7,6},{8,9},{9,8},{10,11... | collective-permute-start | bytes 983048 | tf_op jit(solution)/shard_map/ppermute | solution.py:29
  137.6 1.7 %blend.2.kept = f32[160,1024]{1,0:T(8,128)S(1)} custom-call(bf16[4,160,384]{2,1,0:T(8,128)(2,1)S(1)} %all_to_all.38.got, bf16[4,4,32,2048]{3,2,1,0:T(8,128)(2,1)} %bitcast.8), custom_call_target="tpu_custom_call" | custom-call | tf_op jit(solution)/shard_map/blend/pallas_call | solution.py:56
  139.3 0.0 collective-permute-done.8.arrived
  139.3 0.8 join.1
  (1 shorter events, 0.0 us)
Async XLA Ops:
  6.5 64.4 %all-gather.5.cloned.1.call-start = ((), (), s32[]{:S(2)}) async-start(), calls=%async_computation.7 | async-start | bytes 5898240 | tf_op jit(solution)/shard_map/all_gather | solution.py:471
  8.5 22.1 %copy-start.1 = (bf16[2048,128]{1,0:T(8,128)(2,1)S(1)}, bf16[2048,128]{1,0:T(8,128)(2,1)}, u32[]{:S(2)}) copy-start(bf16[2048,128]{1,0:T(8,128)(2,1)} %query.2) | copy-start | bytes 1572868
  8.5 22.1 %copy-start.3 = (bf16[2048,32]{0,1:T(8,128)(2,1)S(1)}, bf16[2048,32]{0,1:T(8,128)(2,1)}, u32[]{:S(2)}) copy-start(bf16[2048,32]{0,1:T(8,128)(2,1)} %param.11) | copy-start | bytes 393220
  28.6 4.8 %collective-permute-start = (bf16[4,80,2048]{2,1,0:T(8,128)(2,1)S(1)}, bf16[4,80,2048]{2,1,0:T(8,128)(2,1)S(1)}, u32[]{:S(2)}, u32[]{:S(2)}) collective-permute-start(bf16[4,80,2048]{2,1,0:T(8,128)(2,1)S(1)} %all_to_all.35.rows), channel_id=1, source_target_pairs={{0,1},{1,0},{2,3},{3,2},{4,5},{5,4},{6,7},{7,6},{8,9},{9,8},{10,11... | collective-permute-start | bytes 3932168 | tf_op jit(solution)/shard_map/ppermute | solution.py:29
  35.3 9.2 %all-to-all-start.1 = ((bf16[4,160,256]{2,1,0:T(8,128)(2,1)}), bf16[4,160,256]{2,1,0:T(8,128)(2,1)S(1)}, u32[]{:S(2)}, u32[]{:S(2)}) async-start(bf16[4,160,256]{2,1,0:T(8,128)(2,1)} %get-tuple-element.25), calls=%async_computation.1 | async-start | bytes 655360 | tf_op jit(solution)/shard_map/all_to_all | solution.py:24
  38.7 12.6 %copy-start.2 = (bf16[128,2048]{1,0:T(8,128)(2,1)S(1)}, bf16[128,2048]{1,0:T(8,128)(2,1)}, u32[]{:S(2)}) copy-start(bf16[128,2048]{1,0:T(8,128)(2,1)} %shard.1) | copy-start | bytes 1572868
  38.7 22.2 %copy-start.4 = (s32[4,160]{1,0:T(4,128)S(1)}, s32[4,160]{1,0:T(4,128)}, u32[]{:S(2)}) copy-start(s32[4,160]{1,0:T(4,128)} %doc_ids.3) | copy-start | bytes 7684
  45.3 15.6 %all-to-all-start.2 = ((bf16[8,32,160]{2,1,0:T(8,128)(2,1)}), bf16[8,32,160]{2,1,0:T(8,128)(2,1)S(1)}, u32[]{:S(2)}, u32[]{:S(2)}) async-start(bf16[8,32,160]{2,1,0:T(8,128)(2,1)} %get-tuple-element.27), calls=%async_computation.2 | async-start | bytes 262144 | tf_op jit(solution)/shard_map/all_to_all | solution.py:24
  51.4 6.2 %collective-permute-start.1 = (bf16[32,2048]{1,0:T(8,128)(2,1)S(1)}, bf16[32,2048]{1,0:T(8,128)(2,1)S(1)}, u32[]{:S(2)}, u32[]{:S(2)}) collective-permute-start(bf16[32,2048]{1,0:T(8,128)(2,1)S(1)} %get-tuple-element.29), channel_id=1, source_target_pairs={{0,8},{8,16},{16,24},{24,0},{1,9},{9,17},{17,25},{25,1},{2,10},{10... | collective-permute-start | bytes 393224 | tf_op jit(solution)/shard_map/ppermute | solution.py:73
  52.6 8.1 %collective-permute-start.2 = (bf16[32,2048]{1,0:T(8,128)(2,1)S(1)}, bf16[32,2048]{1,0:T(8,128)(2,1)S(1)}, u32[]{:S(2)}, u32[]{:S(2)}) collective-permute-start(bf16[32,2048]{1,0:T(8,128)(2,1)S(1)} %get-tuple-element.30), channel_id=1, source_target_pairs={{0,16},{8,24},{16,0},{24,8},{1,17},{9,25},{17,1},{25,9},{2,18},{10... | collective-permute-start | bytes 393224 | tf_op jit(solution)/shard_map/ppermute | solution.py:73
  52.8 7.8 %collective-permute-start.3 = (bf16[32,2048]{1,0:T(8,128)(2,1)S(1)}, bf16[32,2048]{1,0:T(8,128)(2,1)S(1)}, u32[]{:S(2)}, u32[]{:S(2)}) collective-permute-start(bf16[32,2048]{1,0:T(8,128)(2,1)S(1)} %get-tuple-element.31), channel_id=1, source_target_pairs={{0,24},{8,0},{16,8},{24,16},{1,25},{9,1},{17,9},{25,17},{2,26},{10... | collective-permute-start | bytes 393224 | tf_op jit(solution)/shard_map/ppermute | solution.py:73
  71.9 15.4 %all-to-all-start.4 = ((bf16[4,4,160,128]{3,2,1,0:T(8,128)(2,1)}), bf16[4,4,160,128]{3,2,1,0:T(8,128)(2,1)S(1)}, u32[]{:S(2)}, u32[]{:S(2)}) async-start(bf16[4,4,160,128]{3,2,1,0:T(8,128)(2,1)} %spread.1), calls=%async_computation.4 | async-start | bytes 1310720 | tf_op jit(solution)/shard_map/all_to_all | solution.py:24
  76.4 16.3 %copy-start = (bf16[2048,128]{1,0:T(8,128)(2,1)S(1)}, bf16[2048,128]{1,0:T(8,128)(2,1)}, u32[]{:S(2)}) copy-start(bf16[2048,128]{1,0:T(8,128)(2,1)} %query.3) | copy-start | bytes 1572868
  76.4 57.6 %all-gather.7.cloned.1.call-start = ((), (), s32[]{:S(2)}) async-start(), calls=%async_computation.8 | async-start | bytes 2621440 | tf_op jit(solution)/shard_map/all_gather | solution.py:486
  76.5 5.9 %collective-permute-start.5 = (bf16[32,2048]{1,0:T(8,128)(2,1)S(1)}, bf16[32,2048]{1,0:T(8,128)(2,1)S(1)}, u32[]{:S(2)}, u32[]{:S(2)}) collective-permute-start(bf16[32,2048]{1,0:T(8,128)(2,1)S(1)} %get-tuple-element.34), channel_id=1, source_target_pairs={{0,2},{1,3},{2,4},{3,5},{4,6},{5,7},{6,0},{7,1},{8,10},{9,11},{10,... | collective-permute-start | bytes 393224 | tf_op jit(solution)/shard_map/ppermute | solution.py:73
  76.6 10.5 %collective-permute-start.6 = (bf16[32,2048]{1,0:T(8,128)(2,1)S(1)}, bf16[32,2048]{1,0:T(8,128)(2,1)S(1)}, u32[]{:S(2)}, u32[]{:S(2)}) collective-permute-start(bf16[32,2048]{1,0:T(8,128)(2,1)S(1)} %get-tuple-element.35), channel_id=1, source_target_pairs={{0,4},{1,5},{2,6},{3,7},{4,0},{5,1},{6,2},{7,3},{8,12},{9,13},{10,... | collective-permute-start | bytes 393224 | tf_op jit(solution)/shard_map/ppermute | solution.py:73
  78.3 9.0 %collective-permute-start.7 = (bf16[32,2048]{1,0:T(8,128)(2,1)S(1)}, bf16[32,2048]{1,0:T(8,128)(2,1)S(1)}, u32[]{:S(2)}, u32[]{:S(2)}) collective-permute-start(bf16[32,2048]{1,0:T(8,128)(2,1)S(1)} %get-tuple-element.36), channel_id=1, source_target_pairs={{0,6},{1,7},{2,0},{3,1},{4,2},{5,3},{6,4},{7,5},{8,14},{9,15},{10,... | collective-permute-start | bytes 393224 | tf_op jit(solution)/shard_map/ppermute | solution.py:73
  88.2 4.6 %collective-permute-start.4 = (bf16[4,4,160,128]{3,2,1,0:T(8,128)(2,1)S(1)}, bf16[4,4,160,128]{3,2,1,0:T(8,128)(2,1)S(1)}, u32[]{:S(2)}, u32[]{:S(2)}) collective-permute-start(bf16[4,4,160,128]{3,2,1,0:T(8,128)(2,1)S(1)} %all-to-all-done.4.refs_4_.mine), channel_id=1, source_target_pairs={{0,1},{1,0},{2,3},{3,2},{4,5},{5,4},{6,7},{7,6},{8,9},{9,8},{10,11... | collective-permute-start | bytes 1966088 | tf_op jit(solution)/shard_map/ppermute | solution.py:29
  135.8 3.5 %collective-permute-start.8 = (bf16[160,1024]{1,0:T(8,128)(2,1)S(1)}, bf16[160,1024]{1,0:T(8,128)(2,1)S(1)}, u32[]{:S(2)}, u32[]{:S(2)}) collective-permute-start(bf16[160,1024]{1,0:T(8,128)(2,1)S(1)} %blend.3), channel_id=1, source_target_pairs={{0,1},{1,0},{2,3},{3,2},{4,5},{5,4},{6,7},{7,6},{8,9},{9,8},{10,11... | collective-permute-start | bytes 983048 | tf_op jit(solution)/shard_map/ppermute | solution.py:29
Sparse Core Ops, SparseCore 0:
  9.0 61.3 all-gather.4
  88.3 41.6 all-gather.6

commit v5 on v4

--- a/solution.py
+++ b/solution.py
@@ -481,8 +481,9 @@
     context = first_attend(queries, doc_ids, exchange(keyvals_t, "tp", groups), arrived)
     heads = exchange(context, "tp", core_groups())
     mine = exchange(spread(heads, output_all), "inst")
-    rows_by = stacked(pieces, mine)
-    sums = advance(own_rows, other_rows, mine, other_core(mine), output_all, query_two, rows_by)
+    other = other_core(mine)
+    rows_by = stacked(pieces, other)
+    sums = advance(own_rows, other_rows, mine, other, output_all, query_two, rows_by)
     rows_by = lax.all_gather(rows_by, "inst", axis=0)
 
     sent = second_attend(exchange(sums, "inst"), doc_ids, depth, head)

time: 148 us -> 155 us (1.047)
  blocking collectives: 63.3 us -> 77.9 us
  starting transfers between devices: 27.6 us -> 22.3 us
    all_to_all x4 -> x5, blocking collectives: 63.3 us -> 77.9 us  [exchange(): return lax.all_to_all(block, axis, 0, 0, axis_index_groups=groups)]
    all_to_all x3 -> x2, starting transfers between devices: 14 us -> 9.45 us  [exchange(): return lax.all_to_all(block, axis, 0, 0, axis_index_groups=groups)]
    ppermute x3, waiting for transfers between devices: 2.67 us -> 0.96 us  [other_core(): return lax.ppermute(block, 'tp', [(s, s ^ 1) for s in range(count)])]
    all_to_all x3 -> x2, waiting for transfers between devices: 3.98 us -> 3.96 us  [exchange(): return lax.all_to_all(block, axis, 0, 0, axis_index_groups=groups)]
  transfers between devices with their start and end apart: 14 -> 13, of which waited for: 9 -> 7; matrix products, arithmetic and copies ran while one was open for 0% -> 0% of each run, Pallas kernels for 11% -> 11%
where the time goes in v5:
time: 155 us
  blocking collectives  77.9 us (50%)
  starting transfers between devices  22.3 us (14%)
  Pallas kernels  21.8 us (14%)
  waiting for transfers between devices  19.2 us (12%)
  between operations  13.6 us (9%)
    all_to_all x5, blocking collectives, exchange(): return lax.all_to_all(block, axis, 0, 0, axis_index_groups=groups)  77.9 us
    pallas_call x16, Pallas kernels, call(): pl.pallas_call(kernel, out_shape=outs, in_specs=ins, out_specs=[VMEM if s...  21.8 us
    ppermute x6, waiting for transfers between devices, shifted(): lax.ppermute(block, axis, [(s, (s + distance) % count) for s in range(cou...  14.2 us
    all_to_all x2, starting transfers between devices, exchange(): return lax.all_to_all(block, axis, 0, 0, axis_index_groups=groups)  9.45 us
    ppermute x6, starting transfers between devices, shifted(): lax.ppermute(block, axis, [(s, (s + distance) % count) for s in range(cou...  6.92 us
    ppermute x3, starting transfers between devices, other_core(): return lax.ppermute(block, 'tp', [(s, s ^ 1) for s in range(count)])  5.97 us
    all_to_all x2, waiting for transfers between devices, exchange(): return lax.all_to_all(block, axis, 0, 0, axis_index_groups=groups)  3.96 us
  transfers between devices with their start and end apart: 13, of which 7 were waited for; matrix products, arithmetic and copies ran while one was open for 0% of the time, Pallas kernels for 11%

profile of v5, /device:TPU:1, one launch (start us, length us, event | category | flops | bytes accessed | tf_op | source)
XLA Modules:
  0.0 154.8 jit_solution(13460779878803901159)
XLA Ops:
  6.5 0.0 all-gather.5.cloned.1.call-start
  6.5 2.0 %cut.1 = (bf16[4,80,2048]{2,1,0:T(8,128)(2,1)S(1)}, bf16[160,2048]{1,0:T(8,128)(2,1)}) custom-call(bf16[160,8192]{1,0:T(8,128)(2,1)} %tokens.3, bf16[128,2048]{1,0:T(8,128)(2,1)} %output.1, bf16[32,2048]{1,0:T(8,128)(2,1)} %bitcast.9), custom_call_target="tpu_custom_call" | custom-call | tf_op jit(solution)/shard_map/cut/pallas_call | solution.py:56
  8.5 0.0 all-gather.5.cloned.1.call-update
  8.5 0.0 copy-start.1
  8.6 0.0 copy-start.3
  8.6 20.0 %all_to_all.35.rows = bf16[4,80,2048]{2,1,0:T(8,128)(2,1)S(1)} all-to-all(bf16[4,80,2048]{2,1,0:T(8,128)(2,1)S(1)} %get-tuple-element.21), channel_id=1, replica_groups=mesh['inst'=4,'tp'=8] {'inst'}, dimensions={0} | all-to-all | bytes 2621440 | tf_op jit(solution)/shard_map/all_to_all | solution.py:24
  28.6 2.1 %collective-permute-start = (bf16[4,80,2048]{2,1,0:T(8,128)(2,1)S(1)}, bf16[4,80,2048]{2,1,0:T(8,128)(2,1)S(1)}, u32[]{:S(2)}, u32[]{:S(2)}) collective-permute-start(bf16[4,80,2048]{2,1,0:T(8,128)(2,1)S(1)} %all_to_all.35.rows), channel_id=1, source_target_pairs={{0,1},{1,0},{2,3},{3,2},{4,5},{5,4},{6,7},{7,6},{8,9},{9,8},{10,11... | collective-permute-start | bytes 3932168 | tf_op jit(solution)/shard_map/ppermute | solution.py:29
  30.7 0.0 copy-done.1
  30.7 0.0 copy-done.3
  30.7 0.3 widen.1.weight
  31.0 1.4 project.2
  32.4 1.0 collective-permute-done.rows
  33.3 1.9 %project.3 = (bf16[4,80,2048]{2,1,0:T(8,128)(2,1)}, bf16[4,160,256]{2,1,0:T(8,128)(2,1)}) custom-call(bf16[4,80,2048]{2,1,0:T(8,128)(2,1)S(1)} %collective-permute-done.rows, bf16[2048,256]{1,0:T(8,128)(2,1)S(1)} %widen.1.weight, bf16[4,80,256]{2,1,0:T(8,128)(2,1)S(1)} %get-tuple-element.23.refs_0_), custom_call_target="tpu_custom_call" | custom-call | tf_op jit(solution)/shard_map/project/pallas_call | solution.py:56
  35.3 3.5 %all-to-all-start.1 = ((bf16[4,160,256]{2,1,0:T(8,128)(2,1)}), bf16[4,160,256]{2,1,0:T(8,128)(2,1)S(1)}, u32[]{:S(2)}, u32[]{:S(2)}) async-start(bf16[4,160,256]{2,1,0:T(8,128)(2,1)} %get-tuple-element.25), calls=%async_computation.1 | async-start | bytes 655360 | tf_op jit(solution)/shard_map/all_to_all | solution.py:24
  38.7 0.0 copy-start.2
  38.7 0.0 copy-start.4
  38.8 2.0 %norms.1.scale = f32[160,1]{1,0:T(8,128)S(1)} custom-call(bf16[160,8192]{1,0:T(8,128)(2,1)} %tokens.3), custom_call_target="tpu_custom_call" | custom-call | tf_op jit(solution)/shard_map/norms/pallas_call | solution.py:56
  40.8 3.7 %all-to-all-done.1.parts = bf16[4,160,256]{2,1,0:T(8,128)(2,1)S(1)} async-done(((bf16[4,160,256]{2,1,0:T(8,128)(2,1)}), bf16[4,160,256]{2,1,0:T(8,128)(2,1)S(1)}, u32[]{:S(2)}, u32[]{:S(2)}) %all-to-all-start.1) | async-done | bytes 327712 | tf_op jit(solution)/shard_map/all_to_all | solution.py:24
  44.4 0.9 finish.1
  45.3 6.0 %all-to-all-start.2 = ((bf16[8,32,160]{2,1,0:T(8,128)(2,1)}), bf16[8,32,160]{2,1,0:T(8,128)(2,1)S(1)}, u32[]{:S(2)}, u32[]{:S(2)}) async-start(bf16[8,32,160]{2,1,0:T(8,128)(2,1)} %get-tuple-element.27), calls=%async_computation.2 | async-start | bytes 262144 | tf_op jit(solution)/shard_map/all_to_all | solution.py:24
  51.3 0.0 all-gather.7.cloned.1.call-start
  51.3 0.0 copy-done.2
  51.3 0.1 slices.1
  51.4 1.2 collective-permute-start.1
  52.6 0.3 collective-permute-start.2
  52.9 2.1 %collective-permute-start.3 = (bf16[32,2048]{1,0:T(8,128)(2,1)S(1)}, bf16[32,2048]{1,0:T(8,128)(2,1)S(1)}, u32[]{:S(2)}, u32[]{:S(2)}) collective-permute-start(bf16[32,2048]{1,0:T(8,128)(2,1)S(1)} %get-tuple-element.31), channel_id=1, source_target_pairs={{0,24},{8,0},{16,8},{24,16},{1,25},{9,1},{17,9},{25,17},{2,26},{10... | collective-permute-start | bytes 393224 | tf_op jit(solution)/shard_map/ppermute | solution.py:73
  55.0 2.6 %collective-permute-done.1.refs_1_ = bf16[32,2048]{1,0:T(8,128)(2,1)S(1)} collective-permute-done((bf16[32,2048]{1,0:T(8,128)(2,1)S(1)}, bf16[32,2048]{1,0:T(8,128)(2,1)S(1)}, u32[]{:S(2)}, u32[]{:S(2)}) %collective-permute-start.1) | collective-permute-done | bytes 131104 | tf_op jit(solution)/shard_map/ppermute | solution.py:73
  57.6 3.1 %collective-permute-done.2.refs_2_ = bf16[32,2048]{1,0:T(8,128)(2,1)S(1)} collective-permute-done((bf16[32,2048]{1,0:T(8,128)(2,1)S(1)}, bf16[32,2048]{1,0:T(8,128)(2,1)S(1)}, u32[]{:S(2)}, u32[]{:S(2)}) %collective-permute-start.2) | collective-permute-done | bytes 131104 | tf_op jit(solution)/shard_map/ppermute | solution.py:73
  60.7 0.0 collective-permute-done.3.refs_3_
  60.7 0.3 all-to-all-done.2.pieces
  61.0 0.0 copy-done.4
  61.0 0.5 attend.2
  61.4 9.5 %all_to_all.36.heads = bf16[4,160,128]{2,1,0:T(8,128)(2,1)S(1)} all-to-all(bf16[4,160,128]{2,1,0:T(8,128)(2,1)S(1)} %attend.2), channel_id=1, replica_groups={{0,2,4,6},{1,3,5,7},{8,10,12,14},{9,11,13,15},{16,18,20,22},{17,19,21,2..., dimensions={0} | all-to-all | bytes 327680 | tf_op jit(solution)/shard_map/all_to_all | solution.py:24
  71.0 0.0 all-gather.5.cloned.1.call-done
  71.0 0.1 spread.1
  71.1 13.1 %all_to_all.37.mine = bf16[4,4,160,128]{3,2,1,0:T(8,128)(2,1)S(1)} all-to-all(bf16[4,4,160,128]{3,2,1,0:T(8,128)(2,1)S(1)} %spread.1), channel_id=1, replica_groups=mesh['inst'=4,'tp'=8] {'inst'}, dimensions={0} | all-to-all | bytes 1310720 | tf_op jit(solution)/shard_map/all_to_all | solution.py:24
  84.2 0.0 copy-start
  84.2 2.1 %collective-permute-start.4 = (bf16[4,4,160,128]{3,2,1,0:T(8,128)(2,1)S(1)}, bf16[4,4,160,128]{3,2,1,0:T(8,128)(2,1)S(1)}, u32[]{:S(2)}, u32[]{:S(2)}) collective-permute-start(bf16[4,4,160,128]{3,2,1,0:T(8,128)(2,1)S(1)} %all_to_all.37.mine), channel_id=1, source_target_pairs={{0,1},{1,0},{2,3},{3,2},{4,5},{5,4},{6,7},{7,6},{8,9},{9,8},{10,11... | collective-permute-start | bytes 1966088 | tf_op jit(solution)/shard_map/ppermute | solution.py:29
  86.3 0.1 aim.1
  86.4 0.1 collective-permute-start.5
  86.4 0.8 collective-permute-start.6
  87.2 2.4 %collective-permute-start.7 = (bf16[32,2048]{1,0:T(8,128)(2,1)S(1)}, bf16[32,2048]{1,0:T(8,128)(2,1)S(1)}, u32[]{:S(2)}, u32[]{:S(2)}) collective-permute-start(bf16[32,2048]{1,0:T(8,128)(2,1)S(1)} %get-tuple-element.36), channel_id=1, source_target_pairs={{0,6},{1,7},{2,0},{3,1},{4,2},{5,3},{6,4},{7,5},{8,14},{9,15},{10,... | collective-permute-start | bytes 393224 | tf_op jit(solution)/shard_map/ppermute | solution.py:73
  89.7 3.7 %collective-permute-done.5.refs_1_ = bf16[32,2048]{1,0:T(8,128)(2,1)S(1)} collective-permute-done((bf16[32,2048]{1,0:T(8,128)(2,1)S(1)}, bf16[32,2048]{1,0:T(8,128)(2,1)S(1)}, u32[]{:S(2)}, u32[]{:S(2)}) %collective-permute-start.5) | collective-permute-done | bytes 131104 | tf_op jit(solution)/shard_map/ppermute | solution.py:73
  93.4 4.8 %collective-permute-done.6.refs_2_ = bf16[32,2048]{1,0:T(8,128)(2,1)S(1)} collective-permute-done((bf16[32,2048]{1,0:T(8,128)(2,1)S(1)}, bf16[32,2048]{1,0:T(8,128)(2,1)S(1)}, u32[]{:S(2)}, u32[]{:S(2)}) %collective-permute-start.6) | collective-permute-done | bytes 131104 | tf_op jit(solution)/shard_map/ppermute | solution.py:73
  98.2 0.0 collective-permute-done.7.refs_3_
  98.2 0.0 collective-permute-done.4.refs_4_.other
  98.2 0.9 stack.1.rows_by
  99.0 0.0 all-gather.7.cloned.1.call-update
  99.1 0.0 copy-done
  99.1 6.9 %advance.1 = bf16[4,176,640]{2,1,0:T(8,128)(2,1)S(1)} custom-call(bf16[4,80,2048]{2,1,0:T(8,128)(2,1)} %get-tuple-element.22.own_rows, bf16[4,80,2048]{2,1,0:T(8,128)(2,1)} %get-tuple-element.24.other_rows, bf16[4,4,160,128]{3,2,1,0:T(8,128)(2,1)S(1)} %all_to_all.37.mine, bf16[4,4,160,128]{3,2,1,0:T(8,128)(2,1)S(1)} %collective-permute-done.4.refs_4_.other, ...), custom_call_target="tpu_custom_call" | custom-call | tf_op jit(solution)/shard_map/advance/pallas_call | solution.py:56
  106.0 18.1 %all_to_all.38.parts = bf16[4,176,640]{2,1,0:T(8,128)(2,1)S(1)} all-to-all(bf16[4,176,640]{2,1,0:T(8,128)(2,1)S(1)} %advance.1), channel_id=1, replica_groups=mesh['inst'=4,'tp'=8] {'inst'}, dimensions={0} | all-to-all | bytes 1802240 | tf_op jit(solution)/shard_map/all_to_all | solution.py:24
  124.1 0.6 attend.3
  124.7 17.2 %all_to_all.39.got = bf16[4,160,384]{2,1,0:T(8,128)(2,1)S(1)} all-to-all(bf16[4,160,384]{2,1,0:T(8,128)(2,1)S(1)} %attend.3), channel_id=1, replica_groups={{0,2,4,6},{1,3,5,7},{8,10,12,14},{9,11,13,15},{16,18,20,22},{17,19,21,2..., dimensions={0} | all-to-all | bytes 983040 | tf_op jit(solution)/shard_map/all_to_all | solution.py:24
  141.9 0.0 all-gather.7.cloned.1.call-done
  141.9 1.7 %blend.3 = bf16[160,1024]{1,0:T(8,128)(2,1)S(1)} custom-call(bf16[4,160,384]{2,1,0:T(8,128)(2,1)S(1)} %all_to_all.39.got, bf16[4,4,32,2048]{3,2,1,0:T(8,128)(2,1)} %bitcast.7), custom_call_target="tpu_custom_call" | custom-call | tf_op jit(solution)/shard_map/blend/pallas_call | solution.py:56
  143.7 1.8 %collective-permute-start.8 = (bf16[160,1024]{1,0:T(8,128)(2,1)S(1)}, bf16[160,1024]{1,0:T(8,128)(2,1)S(1)}, u32[]{:S(2)}, u32[]{:S(2)}) collective-permute-start(bf16[160,1024]{1,0:T(8,128)(2,1)S(1)} %blend.3), channel_id=1, source_target_pairs={{0,1},{1,0},{2,3},{3,2},{4,5},{5,4},{6,7},{7,6},{8,9},{9,8},{10,11... | collective-permute-start | bytes 983048 | tf_op jit(solution)/shard_map/ppermute | solution.py:29
  145.4 1.7 %blend.2.kept = f32[160,1024]{1,0:T(8,128)S(1)} custom-call(bf16[4,160,384]{2,1,0:T(8,128)(2,1)S(1)} %all_to_all.39.got, bf16[4,4,32,2048]{3,2,1,0:T(8,128)(2,1)} %bitcast.8), custom_call_target="tpu_custom_call" | custom-call | tf_op jit(solution)/shard_map/blend/pallas_call | solution.py:56
  147.2 0.0 collective-permute-done.8.arrived
  147.2 0.8 join.1
Async XLA Ops:
  6.5 64.4 %all-gather.5.cloned.1.call-start = ((), (), s32[]{:S(2)}) async-start(), calls=%async_computation.7 | async-start | bytes 5898240 | tf_op jit(solution)/shard_map/all_gather | solution.py:471
  8.5 22.1 %copy-start.1 = (bf16[2048,128]{1,0:T(8,128)(2,1)S(1)}, bf16[2048,128]{1,0:T(8,128)(2,1)}, u32[]{:S(2)}) copy-start(bf16[2048,128]{1,0:T(8,128)(2,1)} %query.2) | copy-start | bytes 1572868
  8.6 22.1 %copy-start.3 = (bf16[2048,32]{0,1:T(8,128)(2,1)S(1)}, bf16[2048,32]{0,1:T(8,128)(2,1)}, u32[]{:S(2)}) copy-start(bf16[2048,32]{0,1:T(8,128)(2,1)} %param.11) | copy-start | bytes 393220
  28.6 4.8 %collective-permute-start = (bf16[4,80,2048]{2,1,0:T(8,128)(2,1)S(1)}, bf16[4,80,2048]{2,1,0:T(8,128)(2,1)S(1)}, u32[]{:S(2)}, u32[]{:S(2)}) collective-permute-start(bf16[4,80,2048]{2,1,0:T(8,128)(2,1)S(1)} %all_to_all.35.rows), channel_id=1, source_target_pairs={{0,1},{1,0},{2,3},{3,2},{4,5},{5,4},{6,7},{7,6},{8,9},{9,8},{10,11... | collective-permute-start | bytes 3932168 | tf_op jit(solution)/shard_map/ppermute | solution.py:29
  35.3 9.2 %all-to-all-start.1 = ((bf16[4,160,256]{2,1,0:T(8,128)(2,1)}), bf16[4,160,256]{2,1,0:T(8,128)(2,1)S(1)}, u32[]{:S(2)}, u32[]{:S(2)}) async-start(bf16[4,160,256]{2,1,0:T(8,128)(2,1)} %get-tuple-element.25), calls=%async_computation.1 | async-start | bytes 655360 | tf_op jit(solution)/shard_map/all_to_all | solution.py:24
  38.7 12.6 %copy-start.2 = (bf16[128,2048]{1,0:T(8,128)(2,1)S(1)}, bf16[128,2048]{1,0:T(8,128)(2,1)}, u32[]{:S(2)}) copy-start(bf16[128,2048]{1,0:T(8,128)(2,1)} %shard.1) | copy-start | bytes 1572868
  38.7 22.2 %copy-start.4 = (s32[4,160]{1,0:T(4,128)S(1)}, s32[4,160]{1,0:T(4,128)}, u32[]{:S(2)}) copy-start(s32[4,160]{1,0:T(4,128)} %doc_ids.3) | copy-start | bytes 7684
  45.3 15.6 %all-to-all-start.2 = ((bf16[8,32,160]{2,1,0:T(8,128)(2,1)}), bf16[8,32,160]{2,1,0:T(8,128)(2,1)S(1)}, u32[]{:S(2)}, u32[]{:S(2)}) async-start(bf16[8,32,160]{2,1,0:T(8,128)(2,1)} %get-tuple-element.27), calls=%async_computation.2 | async-start | bytes 262144 | tf_op jit(solution)/shard_map/all_to_all | solution.py:24
  51.3 90.6 %all-gather.7.cloned.1.call-start = ((), (), s32[]{:S(2)}) async-start(), calls=%async_computation.8 | async-start | bytes 2621440 | tf_op jit(solution)/shard_map/all_gather | solution.py:487
  51.4 6.2 %collective-permute-start.1 = (bf16[32,2048]{1,0:T(8,128)(2,1)S(1)}, bf16[32,2048]{1,0:T(8,128)(2,1)S(1)}, u32[]{:S(2)}, u32[]{:S(2)}) collective-permute-start(bf16[32,2048]{1,0:T(8,128)(2,1)S(1)} %get-tuple-element.29), channel_id=1, source_target_pairs={{0,8},{8,16},{16,24},{24,0},{1,9},{9,17},{17,25},{25,1},{2,10},{10... | collective-permute-start | bytes 393224 | tf_op jit(solution)/shard_map/ppermute | solution.py:73
  52.6 8.1 %collective-permute-start.2 = (bf16[32,2048]{1,0:T(8,128)(2,1)S(1)}, bf16[32,2048]{1,0:T(8,128)(2,1)S(1)}, u32[]{:S(2)}, u32[]{:S(2)}) collective-permute-start(bf16[32,2048]{1,0:T(8,128)(2,1)S(1)} %get-tuple-element.30), channel_id=1, source_target_pairs={{0,16},{8,24},{16,0},{24,8},{1,17},{9,25},{17,1},{25,9},{2,18},{10... | collective-permute-start | bytes 393224 | tf_op jit(solution)/shard_map/ppermute | solution.py:73
  52.9 7.8 %collective-permute-start.3 = (bf16[32,2048]{1,0:T(8,128)(2,1)S(1)}, bf16[32,2048]{1,0:T(8,128)(2,1)S(1)}, u32[]{:S(2)}, u32[]{:S(2)}) collective-permute-start(bf16[32,2048]{1,0:T(8,128)(2,1)S(1)} %get-tuple-element.31), channel_id=1, source_target_pairs={{0,24},{8,0},{16,8},{24,16},{1,25},{9,1},{17,9},{25,17},{2,26},{10... | collective-permute-start | bytes 393224 | tf_op jit(solution)/shard_map/ppermute | solution.py:73
  84.2 14.9 %copy-start = (bf16[2048,128]{1,0:T(8,128)(2,1)S(1)}, bf16[2048,128]{1,0:T(8,128)(2,1)}, u32[]{:S(2)}) copy-start(bf16[2048,128]{1,0:T(8,128)(2,1)} %query.3) | copy-start | bytes 1572868
  84.2 14.0 %collective-permute-start.4 = (bf16[4,4,160,128]{3,2,1,0:T(8,128)(2,1)S(1)}, bf16[4,4,160,128]{3,2,1,0:T(8,128)(2,1)S(1)}, u32[]{:S(2)}, u32[]{:S(2)}) collective-permute-start(bf16[4,4,160,128]{3,2,1,0:T(8,128)(2,1)S(1)} %all_to_all.37.mine), channel_id=1, source_target_pairs={{0,1},{1,0},{2,3},{3,2},{4,5},{5,4},{6,7},{7,6},{8,9},{9,8},{10,11... | collective-permute-start | bytes 1966088 | tf_op jit(solution)/shard_map/ppermute | solution.py:29
  86.4 7.0 %collective-permute-start.5 = (bf16[32,2048]{1,0:T(8,128)(2,1)S(1)}, bf16[32,2048]{1,0:T(8,128)(2,1)S(1)}, u32[]{:S(2)}, u32[]{:S(2)}) collective-permute-start(bf16[32,2048]{1,0:T(8,128)(2,1)S(1)} %get-tuple-element.34), channel_id=1, source_target_pairs={{0,2},{1,3},{2,4},{3,5},{4,6},{5,7},{6,0},{7,1},{8,10},{9,11},{10,... | collective-permute-start | bytes 393224 | tf_op jit(solution)/shard_map/ppermute | solution.py:73
  86.4 11.8 %collective-permute-start.6 = (bf16[32,2048]{1,0:T(8,128)(2,1)S(1)}, bf16[32,2048]{1,0:T(8,128)(2,1)S(1)}, u32[]{:S(2)}, u32[]{:S(2)}) collective-permute-start(bf16[32,2048]{1,0:T(8,128)(2,1)S(1)} %get-tuple-element.35), channel_id=1, source_target_pairs={{0,4},{1,5},{2,6},{3,7},{4,0},{5,1},{6,2},{7,3},{8,12},{9,13},{10,... | collective-permute-start | bytes 393224 | tf_op jit(solution)/shard_map/ppermute | solution.py:73
  87.2 10.9 %collective-permute-start.7 = (bf16[32,2048]{1,0:T(8,128)(2,1)S(1)}, bf16[32,2048]{1,0:T(8,128)(2,1)S(1)}, u32[]{:S(2)}, u32[]{:S(2)}) collective-permute-start(bf16[32,2048]{1,0:T(8,128)(2,1)S(1)} %get-tuple-element.36), channel_id=1, source_target_pairs={{0,6},{1,7},{2,0},{3,1},{4,2},{5,3},{6,4},{7,5},{8,14},{9,15},{10,... | collective-permute-start | bytes 393224 | tf_op jit(solution)/shard_map/ppermute | solution.py:73
  143.7 3.5 %collective-permute-start.8 = (bf16[160,1024]{1,0:T(8,128)(2,1)S(1)}, bf16[160,1024]{1,0:T(8,128)(2,1)S(1)}, u32[]{:S(2)}, u32[]{:S(2)}) collective-permute-start(bf16[160,1024]{1,0:T(8,128)(2,1)S(1)} %blend.3), channel_id=1, source_target_pairs={{0,1},{1,0},{2,3},{3,2},{4,5},{5,4},{6,7},{7,6},{8,9},{9,8},{10,11... | collective-permute-start | bytes 983048 | tf_op jit(solution)/shard_map/ppermute | solution.py:29
Sparse Core Ops, SparseCore 0:
  9.0 61.3 all-gather.4
  99.2 42.6 all-gather.6
